TPU v7x, 256 devices: a whole 4x4x8 slice. The times are simulated.
256 devices in a mesh: tm: 32 (over y, x, core), space: 8 (over z).
Axes of the slice: x: 4, y: 4, z: 8, core: 2. Of those that a mesh axis runs over, the one named last changes fastest.
Arguments:
- initial_state: float32 [256, 2048], P('space'), may hold values from -6 to 6
- guesses: float32 [32, 256, 2048], P('tm', 'space'), may hold values from -6 to 6
- diffusivity: float32 [256, 2048], P('space'), may hold values from 0.0125 to 0.025
- forcing_field: float32 [256, 2048], P('space'), may hold values from -1 to 1
- amplitudes: float32 [256], P('tm'), may hold values from 0.5 to 1.5
Outputs:
- corrected: float32 [32, 256, 2048], P('tm', 'space')
All inputs are finite; a program needn't handle non-finite values.
Results may differ from a plain program's by a relative error of at most 0.00002.
Values sent between devices are 32-bit elements; how exact they have to be, the bound alone decides.
A program may use at most 64 MiB of HBM per device.

v0:
```python
import jax
import jax.numpy as jnp
from jax import lax
from jax.sharding import PartitionSpec as P

STEPS = 8


ADVECT = 0.01


def from_behind(value, axis, steps):
    count = lax.axis_size(axis)
    first, last = (max(0, -steps), min(count, count - steps))
    return lax.ppermute(value, axis, [(source, source + steps) for source in range(first, last)])


def with_halo(shard, sides, width):
    for axis, dim in sides:
        count, length = (lax.axis_size(axis), shard.shape[dim])
        up = [(i, (i + 1) % count) for i in range(count - 1)]
        down = [(j, i) for i, j in up]
        last = lax.slice_in_dim(shard, length - width, length, axis=dim)
        first = lax.slice_in_dim(shard, 0, width, axis=dim)
        before = lax.ppermute(last, axis, up)
        after = lax.ppermute(first, axis, down)
        shard = jnp.concatenate([before, shard, after], axis=dim)
    return shard


def advance(padded, diffusivity, factor, forcing):
    center = padded[..., 1:-1, :]
    above_rows = padded[..., :-2, :]
    below_rows = padded[..., 2:, :]
    left_cols = jnp.roll(center, 1, axis=-1)
    right_cols = jnp.roll(center, -1, axis=-1)
    laplace_term = above_rows + below_rows + left_cols + right_cols - 4.0 * center
    return (
        center
        + factor * diffusivity * laplace_term
        - factor * ADVECT * (center - above_rows)
        - factor * ADVECT * (center - left_cols)
        + forcing
    )


def per_device(initial_state, guesses, diffusivity, forcing_field, amplitudes):
    slab_steps = amplitudes.shape[0]
    tm_index = lax.axis_index("tm")
    own_guess = guesses[0]
    arrived = from_behind(own_guess, "tm", 1)
    start_state = jnp.where(tm_index == 0, initial_state, arrived)
    current = start_state
    for k in range(slab_steps):
        padded = with_halo(current, (("space", 0),), 1)
        current = advance(padded, diffusivity, 1.0, amplitudes[k] * forcing_field)
    residual = current - own_guess
    coarse_factor = float(STEPS)
    slab_count = lax.axis_size("tm")
    blank_error = jnp.zeros_like(own_guess)

    def relay_turn(j, error_field):
        incoming = from_behind(error_field, "tm", 1)
        padded_error = with_halo(incoming, (("space", 0),), 1)
        update = advance(padded_error, diffusivity, coarse_factor, 0.0) + residual
        return jnp.where(j == tm_index, update, error_field)

    first_error = jnp.where(tm_index == 0, residual, blank_error)
    correction = lax.fori_loop(1, slab_count, relay_turn, first_error)
    return (own_guess + correction)[None]


def solution(mesh):
    placed = (P("space", None), P("tm", "space", None), P("space", None), P("space", None), P("tm"))
    return jax.shard_map(
        per_device, mesh=mesh, in_specs=placed, out_specs=P("tm", "space", None), check_vma=False
    )
```

profile of v0, /device:TPU:89, one launch (start us, length us, event | category | flops | bytes accessed | tf_op | source)
XLA Modules:
  0.0 665.6 jit_solution(11625812802966666333)
XLA Ops:
  13.1 3.8 collective-permute-done.5
  17.8 4.6 collective-permute-start.6
  78.9 586.0 %while.13 = (s32[]{:T(128)}, f32[32,2048]{1,0:T(8,128)S(1)}, s32[]{:T(128)}, f32[32,2048]{1,0:T(8,128)S(1)}, f32[32,2048]{1,0:T(8,128)S(1)}, /*index=5*/s32[]{:T(128)}) while((s32[]{:T(128)}, f32[32,2048]{1,0:T(8,128)S(1)}, s32[]{:T(128)}, f32[32,2048]{1,0:T(8,128)S(1)}, f32[32,2048]{1,0:T(8,128)S(1)}, /*index=5*/s32[]{:T(128)}) %tuple.72), condition=%wide.region_1.2_spmd, body=%wide.region_0.1_spmd.sunk | while | flops 1310723 | bytes 4047047 | solution.py:69
  78.9 14.0 %collective-permute-start = (f32[32,2048]{1,0:T(8,128)S(1)}, f32[32,2048]{1,0:T(8,128)S(1)}, u32[]{:S(2)}, u32[]{:S(2)}) collective-permute-start(f32[32,2048]{1,0:T(8,128)S(1)} %get-tuple-element.224), channel_id=1, source_target_pairs={{0,8},{8,16},{16,24},{24,32},{32,40},{40,48},{48,56},{56,64},{64,7... | collective-permute-start | bytes 786440 | tf_op jit(solution)/shard_map/while/body/eval_jaxpr/ppermute | solution.py:15
  103.4 5.8 collective-permute-start
  109.2 4.1 collective-permute-done
  120.5 5.0 collective-permute-start
  125.5 6.2 collective-permute-done
  141.0 8.3 %collective-permute-done = f32[32,2048]{1,0:T(8,128)S(1)} collective-permute-done((f32[32,2048]{1,0:T(8,128)S(1)}, f32[32,2048]{1,0:T(8,128)S(1)}, u32[]{:S(2)}, u32[]{:S(2)}) %collective-permute-start) | collective-permute-done | bytes 262176 | tf_op jit(solution)/shard_map/while/body/eval_jaxpr/ppermute | solution.py:15
  151.3 4.6 collective-permute-start.2
  158.9 8.7 %collective-permute-done = f32[32,2048]{1,0:T(8,128)S(1)} collective-permute-done((f32[32,2048]{1,0:T(8,128)S(1)}, f32[32,2048]{1,0:T(8,128)S(1)}, u32[]{:S(2)}, u32[]{:S(2)}) %collective-permute-start) | collective-permute-done | bytes 262176 | tf_op jit(solution)/shard_map/while/body/eval_jaxpr/ppermute | solution.py:15
  169.6 5.1 collective-permute-start.2
  177.7 8.7 %collective-permute-done = f32[32,2048]{1,0:T(8,128)S(1)} collective-permute-done((f32[32,2048]{1,0:T(8,128)S(1)}, f32[32,2048]{1,0:T(8,128)S(1)}, u32[]{:S(2)}, u32[]{:S(2)}) %collective-permute-start) | collective-permute-done | bytes 262176 | tf_op jit(solution)/shard_map/while/body/eval_jaxpr/ppermute | solution.py:15
  188.4 5.1 collective-permute-start.2
  196.5 8.7 %collective-permute-done = f32[32,2048]{1,0:T(8,128)S(1)} collective-permute-done((f32[32,2048]{1,0:T(8,128)S(1)}, f32[32,2048]{1,0:T(8,128)S(1)}, u32[]{:S(2)}, u32[]{:S(2)}) %collective-permute-start) | collective-permute-done | bytes 262176 | tf_op jit(solution)/shard_map/while/body/eval_jaxpr/ppermute | solution.py:15
  207.2 5.1 collective-permute-start.2
  215.4 8.7 %collective-permute-done = f32[32,2048]{1,0:T(8,128)S(1)} collective-permute-done((f32[32,2048]{1,0:T(8,128)S(1)}, f32[32,2048]{1,0:T(8,128)S(1)}, u32[]{:S(2)}, u32[]{:S(2)}) %collective-permute-start) | collective-permute-done | bytes 262176 | tf_op jit(solution)/shard_map/while/body/eval_jaxpr/ppermute | solution.py:15
  226.0 5.1 collective-permute-start.2
  234.2 8.7 %collective-permute-done = f32[32,2048]{1,0:T(8,128)S(1)} collective-permute-done((f32[32,2048]{1,0:T(8,128)S(1)}, f32[32,2048]{1,0:T(8,128)S(1)}, u32[]{:S(2)}, u32[]{:S(2)}) %collective-permute-start) | collective-permute-done | bytes 262176 | tf_op jit(solution)/shard_map/while/body/eval_jaxpr/ppermute | solution.py:15
  244.8 5.1 collective-permute-start.2
  253.0 8.7 %collective-permute-done = f32[32,2048]{1,0:T(8,128)S(1)} collective-permute-done((f32[32,2048]{1,0:T(8,128)S(1)}, f32[32,2048]{1,0:T(8,128)S(1)}, u32[]{:S(2)}, u32[]{:S(2)}) %collective-permute-start) | collective-permute-done | bytes 262176 | tf_op jit(solution)/shard_map/while/body/eval_jaxpr/ppermute | solution.py:15
  263.6 5.1 collective-permute-start.2
  271.8 8.7 %collective-permute-done = f32[32,2048]{1,0:T(8,128)S(1)} collective-permute-done((f32[32,2048]{1,0:T(8,128)S(1)}, f32[32,2048]{1,0:T(8,128)S(1)}, u32[]{:S(2)}, u32[]{:S(2)}) %collective-permute-start) | collective-permute-done | bytes 262176 | tf_op jit(solution)/shard_map/while/body/eval_jaxpr/ppermute | solution.py:15
  282.5 5.1 collective-permute-start.2
  290.6 8.7 %collective-permute-done = f32[32,2048]{1,0:T(8,128)S(1)} collective-permute-done((f32[32,2048]{1,0:T(8,128)S(1)}, f32[32,2048]{1,0:T(8,128)S(1)}, u32[]{:S(2)}, u32[]{:S(2)}) %collective-permute-start) | collective-permute-done | bytes 262176 | tf_op jit(solution)/shard_map/while/body/eval_jaxpr/ppermute | solution.py:15
  301.3 5.1 collective-permute-start.2
  309.4 8.7 %collective-permute-done = f32[32,2048]{1,0:T(8,128)S(1)} collective-permute-done((f32[32,2048]{1,0:T(8,128)S(1)}, f32[32,2048]{1,0:T(8,128)S(1)}, u32[]{:S(2)}, u32[]{:S(2)}) %collective-permute-start) | collective-permute-done | bytes 262176 | tf_op jit(solution)/shard_map/while/body/eval_jaxpr/ppermute | solution.py:15
  320.1 5.1 collective-permute-start.2
  328.2 8.7 %collective-permute-done = f32[32,2048]{1,0:T(8,128)S(1)} collective-permute-done((f32[32,2048]{1,0:T(8,128)S(1)}, f32[32,2048]{1,0:T(8,128)S(1)}, u32[]{:S(2)}, u32[]{:S(2)}) %collective-permute-start) | collective-permute-done | bytes 262176 | tf_op jit(solution)/shard_map/while/body/eval_jaxpr/ppermute | solution.py:15
  338.9 5.1 collective-permute-start.2
  347.0 8.7 %collective-permute-done = f32[32,2048]{1,0:T(8,128)S(1)} collective-permute-done((f32[32,2048]{1,0:T(8,128)S(1)}, f32[32,2048]{1,0:T(8,128)S(1)}, u32[]{:S(2)}, u32[]{:S(2)}) %collective-permute-start) | collective-permute-done | bytes 262176 | tf_op jit(solution)/shard_map/while/body/eval_jaxpr/ppermute | solution.py:15
  357.7 5.1 collective-permute-start.2
  365.8 8.7 %collective-permute-done = f32[32,2048]{1,0:T(8,128)S(1)} collective-permute-done((f32[32,2048]{1,0:T(8,128)S(1)}, f32[32,2048]{1,0:T(8,128)S(1)}, u32[]{:S(2)}, u32[]{:S(2)}) %collective-permute-start) | collective-permute-done | bytes 262176 | tf_op jit(solution)/shard_map/while/body/eval_jaxpr/ppermute | solution.py:15
  376.5 5.1 collective-permute-start.2
  384.7 8.7 %collective-permute-done = f32[32,2048]{1,0:T(8,128)S(1)} collective-permute-done((f32[32,2048]{1,0:T(8,128)S(1)}, f32[32,2048]{1,0:T(8,128)S(1)}, u32[]{:S(2)}, u32[]{:S(2)}) %collective-permute-start) | collective-permute-done | bytes 262176 | tf_op jit(solution)/shard_map/while/body/eval_jaxpr/ppermute | solution.py:15
  395.3 5.1 collective-permute-start.2
  403.5 8.7 %collective-permute-done = f32[32,2048]{1,0:T(8,128)S(1)} collective-permute-done((f32[32,2048]{1,0:T(8,128)S(1)}, f32[32,2048]{1,0:T(8,128)S(1)}, u32[]{:S(2)}, u32[]{:S(2)}) %collective-permute-start) | collective-permute-done | bytes 262176 | tf_op jit(solution)/shard_map/while/body/eval_jaxpr/ppermute | solution.py:15
  414.1 5.1 collective-permute-start.2
  422.3 8.7 %collective-permute-done = f32[32,2048]{1,0:T(8,128)S(1)} collective-permute-done((f32[32,2048]{1,0:T(8,128)S(1)}, f32[32,2048]{1,0:T(8,128)S(1)}, u32[]{:S(2)}, u32[]{:S(2)}) %collective-permute-start) | collective-permute-done | bytes 262176 | tf_op jit(solution)/shard_map/while/body/eval_jaxpr/ppermute | solution.py:15
  432.9 5.1 collective-permute-start.2
  441.1 8.7 %collective-permute-done = f32[32,2048]{1,0:T(8,128)S(1)} collective-permute-done((f32[32,2048]{1,0:T(8,128)S(1)}, f32[32,2048]{1,0:T(8,128)S(1)}, u32[]{:S(2)}, u32[]{:S(2)}) %collective-permute-start) | collective-permute-done | bytes 262176 | tf_op jit(solution)/shard_map/while/body/eval_jaxpr/ppermute | solution.py:15
  451.8 5.1 collective-permute-start.2
  459.9 8.7 %collective-permute-done = f32[32,2048]{1,0:T(8,128)S(1)} collective-permute-done((f32[32,2048]{1,0:T(8,128)S(1)}, f32[32,2048]{1,0:T(8,128)S(1)}, u32[]{:S(2)}, u32[]{:S(2)}) %collective-permute-start) | collective-permute-done | bytes 262176 | tf_op jit(solution)/shard_map/while/body/eval_jaxpr/ppermute | solution.py:15
  470.6 5.1 collective-permute-start.2
  478.7 8.7 %collective-permute-done = f32[32,2048]{1,0:T(8,128)S(1)} collective-permute-done((f32[32,2048]{1,0:T(8,128)S(1)}, f32[32,2048]{1,0:T(8,128)S(1)}, u32[]{:S(2)}, u32[]{:S(2)}) %collective-permute-start) | collective-permute-done | bytes 262176 | tf_op jit(solution)/shard_map/while/body/eval_jaxpr/ppermute | solution.py:15
  489.4 5.1 collective-permute-start.2
  497.5 8.7 %collective-permute-done = f32[32,2048]{1,0:T(8,128)S(1)} collective-permute-done((f32[32,2048]{1,0:T(8,128)S(1)}, f32[32,2048]{1,0:T(8,128)S(1)}, u32[]{:S(2)}, u32[]{:S(2)}) %collective-permute-start) | collective-permute-done | bytes 262176 | tf_op jit(solution)/shard_map/while/body/eval_jaxpr/ppermute | solution.py:15
  508.2 5.1 collective-permute-start.2
  516.3 8.7 %collective-permute-done = f32[32,2048]{1,0:T(8,128)S(1)} collective-permute-done((f32[32,2048]{1,0:T(8,128)S(1)}, f32[32,2048]{1,0:T(8,128)S(1)}, u32[]{:S(2)}, u32[]{:S(2)}) %collective-permute-start) | collective-permute-done | bytes 262176 | tf_op jit(solution)/shard_map/while/body/eval_jaxpr/ppermute | solution.py:15
  527.0 5.1 collective-permute-start.2
  535.1 8.7 %collective-permute-done = f32[32,2048]{1,0:T(8,128)S(1)} collective-permute-done((f32[32,2048]{1,0:T(8,128)S(1)}, f32[32,2048]{1,0:T(8,128)S(1)}, u32[]{:S(2)}, u32[]{:S(2)}) %collective-permute-start) | collective-permute-done | bytes 262176 | tf_op jit(solution)/shard_map/while/body/eval_jaxpr/ppermute | solution.py:15
  545.8 5.1 collective-permute-start.2
  554.0 8.7 %collective-permute-done = f32[32,2048]{1,0:T(8,128)S(1)} collective-permute-done((f32[32,2048]{1,0:T(8,128)S(1)}, f32[32,2048]{1,0:T(8,128)S(1)}, u32[]{:S(2)}, u32[]{:S(2)}) %collective-permute-start) | collective-permute-done | bytes 262176 | tf_op jit(solution)/shard_map/while/body/eval_jaxpr/ppermute | solution.py:15
  564.6 5.1 collective-permute-start.2
  572.8 8.7 %collective-permute-done = f32[32,2048]{1,0:T(8,128)S(1)} collective-permute-done((f32[32,2048]{1,0:T(8,128)S(1)}, f32[32,2048]{1,0:T(8,128)S(1)}, u32[]{:S(2)}, u32[]{:S(2)}) %collective-permute-start) | collective-permute-done | bytes 262176 | tf_op jit(solution)/shard_map/while/body/eval_jaxpr/ppermute | solution.py:15
  583.4 5.1 collective-permute-start.2
  591.6 8.7 %collective-permute-done = f32[32,2048]{1,0:T(8,128)S(1)} collective-permute-done((f32[32,2048]{1,0:T(8,128)S(1)}, f32[32,2048]{1,0:T(8,128)S(1)}, u32[]{:S(2)}, u32[]{:S(2)}) %collective-permute-start) | collective-permute-done | bytes 262176 | tf_op jit(solution)/shard_map/while/body/eval_jaxpr/ppermute | solution.py:15
  602.2 5.1 collective-permute-start.2
  610.4 8.7 %collective-permute-done = f32[32,2048]{1,0:T(8,128)S(1)} collective-permute-done((f32[32,2048]{1,0:T(8,128)S(1)}, f32[32,2048]{1,0:T(8,128)S(1)}, u32[]{:S(2)}, u32[]{:S(2)}) %collective-permute-start) | collective-permute-done | bytes 262176 | tf_op jit(solution)/shard_map/while/body/eval_jaxpr/ppermute | solution.py:15
  621.0 5.1 collective-permute-start.2
  629.2 8.7 %collective-permute-done = f32[32,2048]{1,0:T(8,128)S(1)} collective-permute-done((f32[32,2048]{1,0:T(8,128)S(1)}, f32[32,2048]{1,0:T(8,128)S(1)}, u32[]{:S(2)}, u32[]{:S(2)}) %collective-permute-start) | collective-permute-done | bytes 262176 | tf_op jit(solution)/shard_map/while/body/eval_jaxpr/ppermute | solution.py:15
  639.9 5.1 collective-permute-start.2
  648.0 8.7 %collective-permute-done = f32[32,2048]{1,0:T(8,128)S(1)} collective-permute-done((f32[32,2048]{1,0:T(8,128)S(1)}, f32[32,2048]{1,0:T(8,128)S(1)}, u32[]{:S(2)}, u32[]{:S(2)}) %collective-permute-start) | collective-permute-done | bytes 262176 | tf_op jit(solution)/shard_map/while/body/eval_jaxpr/ppermute | solution.py:15
  658.7 5.1 collective-permute-start.2
  (324 shorter events, 233.2 us)
Async XLA Ops:
  0.0 7.3 %collective-permute-start.3 = (f32[32,2048]{1,0:T(8,128)}, f32[32,2048]{1,0:T(8,128)S(1)}, u32[]{:S(2)}, u32[]{:S(2)}) collective-permute-start(f32[32,2048]{1,0:T(8,128)} %bitcast.14), channel_id=1, source_target_pairs={{0,8},{8,16},{16,24},{24,32},{32,40},{40,48},{48,56},{56,64},{64,7... | collective-permute-start | bytes 786440 | tf_op jit(solution)/shard_map/ppermute | solution.py:15
  17.8 6.6 collective-permute-start.6
  78.9 17.3 %collective-permute-start = (f32[32,2048]{1,0:T(8,128)S(1)}, f32[32,2048]{1,0:T(8,128)S(1)}, u32[]{:S(2)}, u32[]{:S(2)}) collective-permute-start(f32[32,2048]{1,0:T(8,128)S(1)} %get-tuple-element.224), channel_id=1, source_target_pairs={{0,8},{8,16},{16,24},{24,32},{32,40},{40,48},{48,56},{56,64},{64,7... | collective-permute-start | bytes 786440 | tf_op jit(solution)/shard_map/while/body/eval_jaxpr/ppermute | solution.py:15
  103.4 9.9 %collective-permute-start = (f32[32,2048]{1,0:T(8,128)S(1)}, f32[32,2048]{1,0:T(8,128)S(1)}, u32[]{:S(2)}, u32[]{:S(2)}) collective-permute-start(f32[32,2048]{1,0:T(8,128)S(1)} %get-tuple-element.224), channel_id=1, source_target_pairs={{0,8},{8,16},{16,24},{24,32},{32,40},{40,48},{48,56},{56,64},{64,7... | collective-permute-start | bytes 786440 | tf_op jit(solution)/shard_map/while/body/eval_jaxpr/ppermute | solution.py:15
  120.5 11.2 %collective-permute-start = (f32[32,2048]{1,0:T(8,128)S(1)}, f32[32,2048]{1,0:T(8,128)S(1)}, u32[]{:S(2)}, u32[]{:S(2)}) collective-permute-start(f32[32,2048]{1,0:T(8,128)S(1)} %get-tuple-element.224), channel_id=1, source_target_pairs={{0,8},{8,16},{16,24},{24,32},{32,40},{40,48},{48,56},{56,64},{64,7... | collective-permute-start | bytes 786440 | tf_op jit(solution)/shard_map/while/body/eval_jaxpr/ppermute | solution.py:15
  138.5 10.8 %collective-permute-start = (f32[32,2048]{1,0:T(8,128)S(1)}, f32[32,2048]{1,0:T(8,128)S(1)}, u32[]{:S(2)}, u32[]{:S(2)}) collective-permute-start(f32[32,2048]{1,0:T(8,128)S(1)} %get-tuple-element.224), channel_id=1, source_target_pairs={{0,8},{8,16},{16,24},{24,32},{32,40},{40,48},{48,56},{56,64},{64,7... | collective-permute-start | bytes 786440 | tf_op jit(solution)/shard_map/while/body/eval_jaxpr/ppermute | solution.py:15
  149.3 6.8 %collective-permute-start.1 = (f32[1,2048]{1,0:T(1,128)S(1)}, f32[1,2048]{1,0:T(1,128)S(1)}, u32[]{:S(2)}, u32[]{:S(2)}) collective-permute-start(f32[1,2048]{1,0:T(1,128)S(1)} %get-tuple-element.211), channel_id=1, source_target_pairs={{1,0},{2,1},{3,2},{4,3},{5,4},{6,5},{7,6},{9,8},{10,9},{11,10},{12... | collective-permute-start | bytes 24584 | tf_op jit(solution)/shard_map/while/body/eval_jaxpr/ppermute | solution.py:26
  157.0 10.7 %collective-permute-start = (f32[32,2048]{1,0:T(8,128)S(1)}, f32[32,2048]{1,0:T(8,128)S(1)}, u32[]{:S(2)}, u32[]{:S(2)}) collective-permute-start(f32[32,2048]{1,0:T(8,128)S(1)} %get-tuple-element.224), channel_id=1, source_target_pairs={{0,8},{8,16},{16,24},{24,32},{32,40},{40,48},{48,56},{56,64},{64,7... | collective-permute-start | bytes 786440 | tf_op jit(solution)/shard_map/while/body/eval_jaxpr/ppermute | solution.py:15
  167.7 7.3 %collective-permute-start.1 = (f32[1,2048]{1,0:T(1,128)S(1)}, f32[1,2048]{1,0:T(1,128)S(1)}, u32[]{:S(2)}, u32[]{:S(2)}) collective-permute-start(f32[1,2048]{1,0:T(1,128)S(1)} %get-tuple-element.211), channel_id=1, source_target_pairs={{1,0},{2,1},{3,2},{4,3},{5,4},{6,5},{7,6},{9,8},{10,9},{11,10},{12... | collective-permute-start | bytes 24584 | tf_op jit(solution)/shard_map/while/body/eval_jaxpr/ppermute | solution.py:26
  175.8 10.7 %collective-permute-start = (f32[32,2048]{1,0:T(8,128)S(1)}, f32[32,2048]{1,0:T(8,128)S(1)}, u32[]{:S(2)}, u32[]{:S(2)}) collective-permute-start(f32[32,2048]{1,0:T(8,128)S(1)} %get-tuple-element.224), channel_id=1, source_target_pairs={{0,8},{8,16},{16,24},{24,32},{32,40},{40,48},{48,56},{56,64},{64,7... | collective-permute-start | bytes 786440 | tf_op jit(solution)/shard_map/while/body/eval_jaxpr/ppermute | solution.py:15
  186.5 7.3 %collective-permute-start.1 = (f32[1,2048]{1,0:T(1,128)S(1)}, f32[1,2048]{1,0:T(1,128)S(1)}, u32[]{:S(2)}, u32[]{:S(2)}) collective-permute-start(f32[1,2048]{1,0:T(1,128)S(1)} %get-tuple-element.211), channel_id=1, source_target_pairs={{1,0},{2,1},{3,2},{4,3},{5,4},{6,5},{7,6},{9,8},{10,9},{11,10},{12... | collective-permute-start | bytes 24584 | tf_op jit(solution)/shard_map/while/body/eval_jaxpr/ppermute | solution.py:26
  194.6 10.7 %collective-permute-start = (f32[32,2048]{1,0:T(8,128)S(1)}, f32[32,2048]{1,0:T(8,128)S(1)}, u32[]{:S(2)}, u32[]{:S(2)}) collective-permute-start(f32[32,2048]{1,0:T(8,128)S(1)} %get-tuple-element.224), channel_id=1, source_target_pairs={{0,8},{8,16},{16,24},{24,32},{32,40},{40,48},{48,56},{56,64},{64,7... | collective-permute-start | bytes 786440 | tf_op jit(solution)/shard_map/while/body/eval_jaxpr/ppermute | solution.py:15
  205.3 7.3 %collective-permute-start.1 = (f32[1,2048]{1,0:T(1,128)S(1)}, f32[1,2048]{1,0:T(1,128)S(1)}, u32[]{:S(2)}, u32[]{:S(2)}) collective-permute-start(f32[1,2048]{1,0:T(1,128)S(1)} %get-tuple-element.211), channel_id=1, source_target_pairs={{1,0},{2,1},{3,2},{4,3},{5,4},{6,5},{7,6},{9,8},{10,9},{11,10},{12... | collective-permute-start | bytes 24584 | tf_op jit(solution)/shard_map/while/body/eval_jaxpr/ppermute | solution.py:26
  207.2 5.9 collective-permute-start.2
  213.4 10.7 %collective-permute-start = (f32[32,2048]{1,0:T(8,128)S(1)}, f32[32,2048]{1,0:T(8,128)S(1)}, u32[]{:S(2)}, u32[]{:S(2)}) collective-permute-start(f32[32,2048]{1,0:T(8,128)S(1)} %get-tuple-element.224), channel_id=1, source_target_pairs={{0,8},{8,16},{16,24},{24,32},{32,40},{40,48},{48,56},{56,64},{64,7... | collective-permute-start | bytes 786440 | tf_op jit(solution)/shard_map/while/body/eval_jaxpr/ppermute | solution.py:15
  224.1 7.3 %collective-permute-start.1 = (f32[1,2048]{1,0:T(1,128)S(1)}, f32[1,2048]{1,0:T(1,128)S(1)}, u32[]{:S(2)}, u32[]{:S(2)}) collective-permute-start(f32[1,2048]{1,0:T(1,128)S(1)} %get-tuple-element.211), channel_id=1, source_target_pairs={{1,0},{2,1},{3,2},{4,3},{5,4},{6,5},{7,6},{9,8},{10,9},{11,10},{12... | collective-permute-start | bytes 24584 | tf_op jit(solution)/shard_map/while/body/eval_jaxpr/ppermute | solution.py:26
  232.2 10.7 %collective-permute-start = (f32[32,2048]{1,0:T(8,128)S(1)}, f32[32,2048]{1,0:T(8,128)S(1)}, u32[]{:S(2)}, u32[]{:S(2)}) collective-permute-start(f32[32,2048]{1,0:T(8,128)S(1)} %get-tuple-element.224), channel_id=1, source_target_pairs={{0,8},{8,16},{16,24},{24,32},{32,40},{40,48},{48,56},{56,64},{64,7... | collective-permute-start | bytes 786440 | tf_op jit(solution)/shard_map/while/body/eval_jaxpr/ppermute | solution.py:15
  242.9 7.3 %collective-permute-start.1 = (f32[1,2048]{1,0:T(1,128)S(1)}, f32[1,2048]{1,0:T(1,128)S(1)}, u32[]{:S(2)}, u32[]{:S(2)}) collective-permute-start(f32[1,2048]{1,0:T(1,128)S(1)} %get-tuple-element.211), channel_id=1, source_target_pairs={{1,0},{2,1},{3,2},{4,3},{5,4},{6,5},{7,6},{9,8},{10,9},{11,10},{12... | collective-permute-start | bytes 24584 | tf_op jit(solution)/shard_map/while/body/eval_jaxpr/ppermute | solution.py:26
  251.0 10.7 %collective-permute-start = (f32[32,2048]{1,0:T(8,128)S(1)}, f32[32,2048]{1,0:T(8,128)S(1)}, u32[]{:S(2)}, u32[]{:S(2)}) collective-permute-start(f32[32,2048]{1,0:T(8,128)S(1)} %get-tuple-element.224), channel_id=1, source_target_pairs={{0,8},{8,16},{16,24},{24,32},{32,40},{40,48},{48,56},{56,64},{64,7... | collective-permute-start | bytes 786440 | tf_op jit(solution)/shard_map/while/body/eval_jaxpr/ppermute | solution.py:15
  261.7 7.3 %collective-permute-start.1 = (f32[1,2048]{1,0:T(1,128)S(1)}, f32[1,2048]{1,0:T(1,128)S(1)}, u32[]{:S(2)}, u32[]{:S(2)}) collective-permute-start(f32[1,2048]{1,0:T(1,128)S(1)} %get-tuple-element.211), channel_id=1, source_target_pairs={{1,0},{2,1},{3,2},{4,3},{5,4},{6,5},{7,6},{9,8},{10,9},{11,10},{12... | collective-permute-start | bytes 24584 | tf_op jit(solution)/shard_map/while/body/eval_jaxpr/ppermute | solution.py:26
  263.6 5.9 collective-permute-start.2
  269.9 10.7 %collective-permute-start = (f32[32,2048]{1,0:T(8,128)S(1)}, f32[32,2048]{1,0:T(8,128)S(1)}, u32[]{:S(2)}, u32[]{:S(2)}) collective-permute-start(f32[32,2048]{1,0:T(8,128)S(1)} %get-tuple-element.224), channel_id=1, source_target_pairs={{0,8},{8,16},{16,24},{24,32},{32,40},{40,48},{48,56},{56,64},{64,7... | collective-permute-start | bytes 786440 | tf_op jit(solution)/shard_map/while/body/eval_jaxpr/ppermute | solution.py:15
  280.5 7.3 %collective-permute-start.1 = (f32[1,2048]{1,0:T(1,128)S(1)}, f32[1,2048]{1,0:T(1,128)S(1)}, u32[]{:S(2)}, u32[]{:S(2)}) collective-permute-start(f32[1,2048]{1,0:T(1,128)S(1)} %get-tuple-element.211), channel_id=1, source_target_pairs={{1,0},{2,1},{3,2},{4,3},{5,4},{6,5},{7,6},{9,8},{10,9},{11,10},{12... | collective-permute-start | bytes 24584 | tf_op jit(solution)/shard_map/while/body/eval_jaxpr/ppermute | solution.py:26
  288.7 10.7 %collective-permute-start = (f32[32,2048]{1,0:T(8,128)S(1)}, f32[32,2048]{1,0:T(8,128)S(1)}, u32[]{:S(2)}, u32[]{:S(2)}) collective-permute-start(f32[32,2048]{1,0:T(8,128)S(1)} %get-tuple-element.224), channel_id=1, source_target_pairs={{0,8},{8,16},{16,24},{24,32},{32,40},{40,48},{48,56},{56,64},{64,7... | collective-permute-start | bytes 786440 | tf_op jit(solution)/shard_map/while/body/eval_jaxpr/ppermute | solution.py:15
  299.3 7.3 %collective-permute-start.1 = (f32[1,2048]{1,0:T(1,128)S(1)}, f32[1,2048]{1,0:T(1,128)S(1)}, u32[]{:S(2)}, u32[]{:S(2)}) collective-permute-start(f32[1,2048]{1,0:T(1,128)S(1)} %get-tuple-element.211), channel_id=1, source_target_pairs={{1,0},{2,1},{3,2},{4,3},{5,4},{6,5},{7,6},{9,8},{10,9},{11,10},{12... | collective-permute-start | bytes 24584 | tf_op jit(solution)/shard_map/while/body/eval_jaxpr/ppermute | solution.py:26
  307.5 10.7 %collective-permute-start = (f32[32,2048]{1,0:T(8,128)S(1)}, f32[32,2048]{1,0:T(8,128)S(1)}, u32[]{:S(2)}, u32[]{:S(2)}) collective-permute-start(f32[32,2048]{1,0:T(8,128)S(1)} %get-tuple-element.224), channel_id=1, source_target_pairs={{0,8},{8,16},{16,24},{24,32},{32,40},{40,48},{48,56},{56,64},{64,7... | collective-permute-start | bytes 786440 | tf_op jit(solution)/shard_map/while/body/eval_jaxpr/ppermute | solution.py:15
  318.1 7.3 %collective-permute-start.1 = (f32[1,2048]{1,0:T(1,128)S(1)}, f32[1,2048]{1,0:T(1,128)S(1)}, u32[]{:S(2)}, u32[]{:S(2)}) collective-permute-start(f32[1,2048]{1,0:T(1,128)S(1)} %get-tuple-element.211), channel_id=1, source_target_pairs={{1,0},{2,1},{3,2},{4,3},{5,4},{6,5},{7,6},{9,8},{10,9},{11,10},{12... | collective-permute-start | bytes 24584 | tf_op jit(solution)/shard_map/while/body/eval_jaxpr/ppermute | solution.py:26
  326.3 10.7 %collective-permute-start = (f32[32,2048]{1,0:T(8,128)S(1)}, f32[32,2048]{1,0:T(8,128)S(1)}, u32[]{:S(2)}, u32[]{:S(2)}) collective-permute-start(f32[32,2048]{1,0:T(8,128)S(1)} %get-tuple-element.224), channel_id=1, source_target_pairs={{0,8},{8,16},{16,24},{24,32},{32,40},{40,48},{48,56},{56,64},{64,7... | collective-permute-start | bytes 786440 | tf_op jit(solution)/shard_map/while/body/eval_jaxpr/ppermute | solution.py:15
  337.0 7.3 %collective-permute-start.1 = (f32[1,2048]{1,0:T(1,128)S(1)}, f32[1,2048]{1,0:T(1,128)S(1)}, u32[]{:S(2)}, u32[]{:S(2)}) collective-permute-start(f32[1,2048]{1,0:T(1,128)S(1)} %get-tuple-element.211), channel_id=1, source_target_pairs={{1,0},{2,1},{3,2},{4,3},{5,4},{6,5},{7,6},{9,8},{10,9},{11,10},{12... | collective-permute-start | bytes 24584 | tf_op jit(solution)/shard_map/while/body/eval_jaxpr/ppermute | solution.py:26
  345.1 10.7 %collective-permute-start = (f32[32,2048]{1,0:T(8,128)S(1)}, f32[32,2048]{1,0:T(8,128)S(1)}, u32[]{:S(2)}, u32[]{:S(2)}) collective-permute-start(f32[32,2048]{1,0:T(8,128)S(1)} %get-tuple-element.224), channel_id=1, source_target_pairs={{0,8},{8,16},{16,24},{24,32},{32,40},{40,48},{48,56},{56,64},{64,7... | collective-permute-start | bytes 786440 | tf_op jit(solution)/shard_map/while/body/eval_jaxpr/ppermute | solution.py:15
  355.8 7.3 %collective-permute-start.1 = (f32[1,2048]{1,0:T(1,128)S(1)}, f32[1,2048]{1,0:T(1,128)S(1)}, u32[]{:S(2)}, u32[]{:S(2)}) collective-permute-start(f32[1,2048]{1,0:T(1,128)S(1)} %get-tuple-element.211), channel_id=1, source_target_pairs={{1,0},{2,1},{3,2},{4,3},{5,4},{6,5},{7,6},{9,8},{10,9},{11,10},{12... | collective-permute-start | bytes 24584 | tf_op jit(solution)/shard_map/while/body/eval_jaxpr/ppermute | solution.py:26
  357.7 5.9 collective-permute-start.2
  363.9 10.7 %collective-permute-start = (f32[32,2048]{1,0:T(8,128)S(1)}, f32[32,2048]{1,0:T(8,128)S(1)}, u32[]{:S(2)}, u32[]{:S(2)}) collective-permute-start(f32[32,2048]{1,0:T(8,128)S(1)} %get-tuple-element.224), channel_id=1, source_target_pairs={{0,8},{8,16},{16,24},{24,32},{32,40},{40,48},{48,56},{56,64},{64,7... | collective-permute-start | bytes 786440 | tf_op jit(solution)/shard_map/while/body/eval_jaxpr/ppermute | solution.py:15
  374.6 7.3 %collective-permute-start.1 = (f32[1,2048]{1,0:T(1,128)S(1)}, f32[1,2048]{1,0:T(1,128)S(1)}, u32[]{:S(2)}, u32[]{:S(2)}) collective-permute-start(f32[1,2048]{1,0:T(1,128)S(1)} %get-tuple-element.211), channel_id=1, source_target_pairs={{1,0},{2,1},{3,2},{4,3},{5,4},{6,5},{7,6},{9,8},{10,9},{11,10},{12... | collective-permute-start | bytes 24584 | tf_op jit(solution)/shard_map/while/body/eval_jaxpr/ppermute | solution.py:26
  382.7 10.7 %collective-permute-start = (f32[32,2048]{1,0:T(8,128)S(1)}, f32[32,2048]{1,0:T(8,128)S(1)}, u32[]{:S(2)}, u32[]{:S(2)}) collective-permute-start(f32[32,2048]{1,0:T(8,128)S(1)} %get-tuple-element.224), channel_id=1, source_target_pairs={{0,8},{8,16},{16,24},{24,32},{32,40},{40,48},{48,56},{56,64},{64,7... | collective-permute-start | bytes 786440 | tf_op jit(solution)/shard_map/while/body/eval_jaxpr/ppermute | solution.py:15
  393.4 7.3 %collective-permute-start.1 = (f32[1,2048]{1,0:T(1,128)S(1)}, f32[1,2048]{1,0:T(1,128)S(1)}, u32[]{:S(2)}, u32[]{:S(2)}) collective-permute-start(f32[1,2048]{1,0:T(1,128)S(1)} %get-tuple-element.211), channel_id=1, source_target_pairs={{1,0},{2,1},{3,2},{4,3},{5,4},{6,5},{7,6},{9,8},{10,9},{11,10},{12... | collective-permute-start | bytes 24584 | tf_op jit(solution)/shard_map/while/body/eval_jaxpr/ppermute | solution.py:26
  401.5 10.7 %collective-permute-start = (f32[32,2048]{1,0:T(8,128)S(1)}, f32[32,2048]{1,0:T(8,128)S(1)}, u32[]{:S(2)}, u32[]{:S(2)}) collective-permute-start(f32[32,2048]{1,0:T(8,128)S(1)} %get-tuple-element.224), channel_id=1, source_target_pairs={{0,8},{8,16},{16,24},{24,32},{32,40},{40,48},{48,56},{56,64},{64,7... | collective-permute-start | bytes 786440 | tf_op jit(solution)/shard_map/while/body/eval_jaxpr/ppermute | solution.py:15
  412.2 7.3 %collective-permute-start.1 = (f32[1,2048]{1,0:T(1,128)S(1)}, f32[1,2048]{1,0:T(1,128)S(1)}, u32[]{:S(2)}, u32[]{:S(2)}) collective-permute-start(f32[1,2048]{1,0:T(1,128)S(1)} %get-tuple-element.211), channel_id=1, source_target_pairs={{1,0},{2,1},{3,2},{4,3},{5,4},{6,5},{7,6},{9,8},{10,9},{11,10},{12... | collective-permute-start | bytes 24584 | tf_op jit(solution)/shard_map/while/body/eval_jaxpr/ppermute | solution.py:26
  420.3 10.7 %collective-permute-start = (f32[32,2048]{1,0:T(8,128)S(1)}, f32[32,2048]{1,0:T(8,128)S(1)}, u32[]{:S(2)}, u32[]{:S(2)}) collective-permute-start(f32[32,2048]{1,0:T(8,128)S(1)} %get-tuple-element.224), channel_id=1, source_target_pairs={{0,8},{8,16},{16,24},{24,32},{32,40},{40,48},{48,56},{56,64},{64,7... | collective-permute-start | bytes 786440 | tf_op jit(solution)/shard_map/while/body/eval_jaxpr/ppermute | solution.py:15
  431.0 7.3 %collective-permute-start.1 = (f32[1,2048]{1,0:T(1,128)S(1)}, f32[1,2048]{1,0:T(1,128)S(1)}, u32[]{:S(2)}, u32[]{:S(2)}) collective-permute-start(f32[1,2048]{1,0:T(1,128)S(1)} %get-tuple-element.211), channel_id=1, source_target_pairs={{1,0},{2,1},{3,2},{4,3},{5,4},{6,5},{7,6},{9,8},{10,9},{11,10},{12... | collective-permute-start | bytes 24584 | tf_op jit(solution)/shard_map/while/body/eval_jaxpr/ppermute | solution.py:26
  439.1 10.7 %collective-permute-start = (f32[32,2048]{1,0:T(8,128)S(1)}, f32[32,2048]{1,0:T(8,128)S(1)}, u32[]{:S(2)}, u32[]{:S(2)}) collective-permute-start(f32[32,2048]{1,0:T(8,128)S(1)} %get-tuple-element.224), channel_id=1, source_target_pairs={{0,8},{8,16},{16,24},{24,32},{32,40},{40,48},{48,56},{56,64},{64,7... | collective-permute-start | bytes 786440 | tf_op jit(solution)/shard_map/while/body/eval_jaxpr/ppermute | solution.py:15
  449.8 7.3 %collective-permute-start.1 = (f32[1,2048]{1,0:T(1,128)S(1)}, f32[1,2048]{1,0:T(1,128)S(1)}, u32[]{:S(2)}, u32[]{:S(2)}) collective-permute-start(f32[1,2048]{1,0:T(1,128)S(1)} %get-tuple-element.211), channel_id=1, source_target_pairs={{1,0},{2,1},{3,2},{4,3},{5,4},{6,5},{7,6},{9,8},{10,9},{11,10},{12... | collective-permute-start | bytes 24584 | tf_op jit(solution)/shard_map/while/body/eval_jaxpr/ppermute | solution.py:26
  458.0 10.7 %collective-permute-start = (f32[32,2048]{1,0:T(8,128)S(1)}, f32[32,2048]{1,0:T(8,128)S(1)}, u32[]{:S(2)}, u32[]{:S(2)}) collective-permute-start(f32[32,2048]{1,0:T(8,128)S(1)} %get-tuple-element.224), channel_id=1, source_target_pairs={{0,8},{8,16},{16,24},{24,32},{32,40},{40,48},{48,56},{56,64},{64,7... | collective-permute-start | bytes 786440 | tf_op jit(solution)/shard_map/while/body/eval_jaxpr/ppermute | solution.py:15
  468.6 7.3 %collective-permute-start.1 = (f32[1,2048]{1,0:T(1,128)S(1)}, f32[1,2048]{1,0:T(1,128)S(1)}, u32[]{:S(2)}, u32[]{:S(2)}) collective-permute-start(f32[1,2048]{1,0:T(1,128)S(1)} %get-tuple-element.211), channel_id=1, source_target_pairs={{1,0},{2,1},{3,2},{4,3},{5,4},{6,5},{7,6},{9,8},{10,9},{11,10},{12... | collective-permute-start | bytes 24584 | tf_op jit(solution)/shard_map/while/body/eval_jaxpr/ppermute | solution.py:26
  476.8 10.7 %collective-permute-start = (f32[32,2048]{1,0:T(8,128)S(1)}, f32[32,2048]{1,0:T(8,128)S(1)}, u32[]{:S(2)}, u32[]{:S(2)}) collective-permute-start(f32[32,2048]{1,0:T(8,128)S(1)} %get-tuple-element.224), channel_id=1, source_target_pairs={{0,8},{8,16},{16,24},{24,32},{32,40},{40,48},{48,56},{56,64},{64,7... | collective-permute-start | bytes 786440 | tf_op jit(solution)/shard_map/while/body/eval_jaxpr/ppermute | solution.py:15
  487.4 7.3 %collective-permute-start.1 = (f32[1,2048]{1,0:T(1,128)S(1)}, f32[1,2048]{1,0:T(1,128)S(1)}, u32[]{:S(2)}, u32[]{:S(2)}) collective-permute-start(f32[1,2048]{1,0:T(1,128)S(1)} %get-tuple-element.211), channel_id=1, source_target_pairs={{1,0},{2,1},{3,2},{4,3},{5,4},{6,5},{7,6},{9,8},{10,9},{11,10},{12... | collective-permute-start | bytes 24584 | tf_op jit(solution)/shard_map/while/body/eval_jaxpr/ppermute | solution.py:26
  495.6 10.7 %collective-permute-start = (f32[32,2048]{1,0:T(8,128)S(1)}, f32[32,2048]{1,0:T(8,128)S(1)}, u32[]{:S(2)}, u32[]{:S(2)}) collective-permute-start(f32[32,2048]{1,0:T(8,128)S(1)} %get-tuple-element.224), channel_id=1, source_target_pairs={{0,8},{8,16},{16,24},{24,32},{32,40},{40,48},{48,56},{56,64},{64,7... | collective-permute-start | bytes 786440 | tf_op jit(solution)/shard_map/while/body/eval_jaxpr/ppermute | solution.py:15
  506.3 7.3 %collective-permute-start.1 = (f32[1,2048]{1,0:T(1,128)S(1)}, f32[1,2048]{1,0:T(1,128)S(1)}, u32[]{:S(2)}, u32[]{:S(2)}) collective-permute-start(f32[1,2048]{1,0:T(1,128)S(1)} %get-tuple-element.211), channel_id=1, source_target_pairs={{1,0},{2,1},{3,2},{4,3},{5,4},{6,5},{7,6},{9,8},{10,9},{11,10},{12... | collective-permute-start | bytes 24584 | tf_op jit(solution)/shard_map/while/body/eval_jaxpr/ppermute | solution.py:26
  514.4 10.7 %collective-permute-start = (f32[32,2048]{1,0:T(8,128)S(1)}, f32[32,2048]{1,0:T(8,128)S(1)}, u32[]{:S(2)}, u32[]{:S(2)}) collective-permute-start(f32[32,2048]{1,0:T(8,128)S(1)} %get-tuple-element.224), channel_id=1, source_target_pairs={{0,8},{8,16},{16,24},{24,32},{32,40},{40,48},{48,56},{56,64},{64,7... | collective-permute-start | bytes 786440 | tf_op jit(solution)/shard_map/while/body/eval_jaxpr/ppermute | solution.py:15
  525.1 7.3 %collective-permute-start.1 = (f32[1,2048]{1,0:T(1,128)S(1)}, f32[1,2048]{1,0:T(1,128)S(1)}, u32[]{:S(2)}, u32[]{:S(2)}) collective-permute-start(f32[1,2048]{1,0:T(1,128)S(1)} %get-tuple-element.211), channel_id=1, source_target_pairs={{1,0},{2,1},{3,2},{4,3},{5,4},{6,5},{7,6},{9,8},{10,9},{11,10},{12... | collective-permute-start | bytes 24584 | tf_op jit(solution)/shard_map/while/body/eval_jaxpr/ppermute | solution.py:26
  533.2 10.7 %collective-permute-start = (f32[32,2048]{1,0:T(8,128)S(1)}, f32[32,2048]{1,0:T(8,128)S(1)}, u32[]{:S(2)}, u32[]{:S(2)}) collective-permute-start(f32[32,2048]{1,0:T(8,128)S(1)} %get-tuple-element.224), channel_id=1, source_target_pairs={{0,8},{8,16},{16,24},{24,32},{32,40},{40,48},{48,56},{56,64},{64,7... | collective-permute-start | bytes 786440 | tf_op jit(solution)/shard_map/while/body/eval_jaxpr/ppermute | solution.py:15
  543.9 7.3 %collective-permute-start.1 = (f32[1,2048]{1,0:T(1,128)S(1)}, f32[1,2048]{1,0:T(1,128)S(1)}, u32[]{:S(2)}, u32[]{:S(2)}) collective-permute-start(f32[1,2048]{1,0:T(1,128)S(1)} %get-tuple-element.211), channel_id=1, source_target_pairs={{1,0},{2,1},{3,2},{4,3},{5,4},{6,5},{7,6},{9,8},{10,9},{11,10},{12... | collective-permute-start | bytes 24584 | tf_op jit(solution)/shard_map/while/body/eval_jaxpr/ppermute | solution.py:26
  552.0 10.7 %collective-permute-start = (f32[32,2048]{1,0:T(8,128)S(1)}, f32[32,2048]{1,0:T(8,128)S(1)}, u32[]{:S(2)}, u32[]{:S(2)}) collective-permute-start(f32[32,2048]{1,0:T(8,128)S(1)} %get-tuple-element.224), channel_id=1, source_target_pairs={{0,8},{8,16},{16,24},{24,32},{32,40},{40,48},{48,56},{56,64},{64,7... | collective-permute-start | bytes 786440 | tf_op jit(solution)/shard_map/while/body/eval_jaxpr/ppermute | solution.py:15
  562.7 7.3 %collective-permute-start.1 = (f32[1,2048]{1,0:T(1,128)S(1)}, f32[1,2048]{1,0:T(1,128)S(1)}, u32[]{:S(2)}, u32[]{:S(2)}) collective-permute-start(f32[1,2048]{1,0:T(1,128)S(1)} %get-tuple-element.211), channel_id=1, source_target_pairs={{1,0},{2,1},{3,2},{4,3},{5,4},{6,5},{7,6},{9,8},{10,9},{11,10},{12... | collective-permute-start | bytes 24584 | tf_op jit(solution)/shard_map/while/body/eval_jaxpr/ppermute | solution.py:26
  570.8 10.7 %collective-permute-start = (f32[32,2048]{1,0:T(8,128)S(1)}, f32[32,2048]{1,0:T(8,128)S(1)}, u32[]{:S(2)}, u32[]{:S(2)}) collective-permute-start(f32[32,2048]{1,0:T(8,128)S(1)} %get-tuple-element.224), channel_id=1, source_target_pairs={{0,8},{8,16},{16,24},{24,32},{32,40},{40,48},{48,56},{56,64},{64,7... | collective-permute-start | bytes 786440 | tf_op jit(solution)/shard_map/while/body/eval_jaxpr/ppermute | solution.py:15
  581.5 7.3 %collective-permute-start.1 = (f32[1,2048]{1,0:T(1,128)S(1)}, f32[1,2048]{1,0:T(1,128)S(1)}, u32[]{:S(2)}, u32[]{:S(2)}) collective-permute-start(f32[1,2048]{1,0:T(1,128)S(1)} %get-tuple-element.211), channel_id=1, source_target_pairs={{1,0},{2,1},{3,2},{4,3},{5,4},{6,5},{7,6},{9,8},{10,9},{11,10},{12... | collective-permute-start | bytes 24584 | tf_op jit(solution)/shard_map/while/body/eval_jaxpr/ppermute | solution.py:26
  589.6 10.7 %collective-permute-start = (f32[32,2048]{1,0:T(8,128)S(1)}, f32[32,2048]{1,0:T(8,128)S(1)}, u32[]{:S(2)}, u32[]{:S(2)}) collective-permute-start(f32[32,2048]{1,0:T(8,128)S(1)} %get-tuple-element.224), channel_id=1, source_target_pairs={{0,8},{8,16},{16,24},{24,32},{32,40},{40,48},{48,56},{56,64},{64,7... | collective-permute-start | bytes 786440 | tf_op jit(solution)/shard_map/while/body/eval_jaxpr/ppermute | solution.py:15
  600.3 7.3 %collective-permute-start.1 = (f32[1,2048]{1,0:T(1,128)S(1)}, f32[1,2048]{1,0:T(1,128)S(1)}, u32[]{:S(2)}, u32[]{:S(2)}) collective-permute-start(f32[1,2048]{1,0:T(1,128)S(1)} %get-tuple-element.211), channel_id=1, source_target_pairs={{1,0},{2,1},{3,2},{4,3},{5,4},{6,5},{7,6},{9,8},{10,9},{11,10},{12... | collective-permute-start | bytes 24584 | tf_op jit(solution)/shard_map/while/body/eval_jaxpr/ppermute | solution.py:26
  608.4 10.7 %collective-permute-start = (f32[32,2048]{1,0:T(8,128)S(1)}, f32[32,2048]{1,0:T(8,128)S(1)}, u32[]{:S(2)}, u32[]{:S(2)}) collective-permute-start(f32[32,2048]{1,0:T(8,128)S(1)} %get-tuple-element.224), channel_id=1, source_target_pairs={{0,8},{8,16},{16,24},{24,32},{32,40},{40,48},{48,56},{56,64},{64,7... | collective-permute-start | bytes 786440 | tf_op jit(solution)/shard_map/while/body/eval_jaxpr/ppermute | solution.py:15
  619.1 7.3 %collective-permute-start.1 = (f32[1,2048]{1,0:T(1,128)S(1)}, f32[1,2048]{1,0:T(1,128)S(1)}, u32[]{:S(2)}, u32[]{:S(2)}) collective-permute-start(f32[1,2048]{1,0:T(1,128)S(1)} %get-tuple-element.211), channel_id=1, source_target_pairs={{1,0},{2,1},{3,2},{4,3},{5,4},{6,5},{7,6},{9,8},{10,9},{11,10},{12... | collective-permute-start | bytes 24584 | tf_op jit(solution)/shard_map/while/body/eval_jaxpr/ppermute | solution.py:26
  627.3 10.7 %collective-permute-start = (f32[32,2048]{1,0:T(8,128)S(1)}, f32[32,2048]{1,0:T(8,128)S(1)}, u32[]{:S(2)}, u32[]{:S(2)}) collective-permute-start(f32[32,2048]{1,0:T(8,128)S(1)} %get-tuple-element.224), channel_id=1, source_target_pairs={{0,8},{8,16},{16,24},{24,32},{32,40},{40,48},{48,56},{56,64},{64,7... | collective-permute-start | bytes 786440 | tf_op jit(solution)/shard_map/while/body/eval_jaxpr/ppermute | solution.py:15
  637.9 7.3 %collective-permute-start.1 = (f32[1,2048]{1,0:T(1,128)S(1)}, f32[1,2048]{1,0:T(1,128)S(1)}, u32[]{:S(2)}, u32[]{:S(2)}) collective-permute-start(f32[1,2048]{1,0:T(1,128)S(1)} %get-tuple-element.211), channel_id=1, source_target_pairs={{1,0},{2,1},{3,2},{4,3},{5,4},{6,5},{7,6},{9,8},{10,9},{11,10},{12... | collective-permute-start | bytes 24584 | tf_op jit(solution)/shard_map/while/body/eval_jaxpr/ppermute | solution.py:26
  646.1 10.7 %collective-permute-start = (f32[32,2048]{1,0:T(8,128)S(1)}, f32[32,2048]{1,0:T(8,128)S(1)}, u32[]{:S(2)}, u32[]{:S(2)}) collective-permute-start(f32[32,2048]{1,0:T(8,128)S(1)} %get-tuple-element.224), channel_id=1, source_target_pairs={{0,8},{8,16},{16,24},{24,32},{32,40},{40,48},{48,56},{56,64},{64,7... | collective-permute-start | bytes 786440 | tf_op jit(solution)/shard_map/while/body/eval_jaxpr/ppermute | solution.py:15
  656.7 7.3 %collective-permute-start.1 = (f32[1,2048]{1,0:T(1,128)S(1)}, f32[1,2048]{1,0:T(1,128)S(1)}, u32[]{:S(2)}, u32[]{:S(2)}) collective-permute-start(f32[1,2048]{1,0:T(1,128)S(1)} %get-tuple-element.211), channel_id=1, source_target_pairs={{1,0},{2,1},{3,2},{4,3},{5,4},{6,5},{7,6},{9,8},{10,9},{11,10},{12... | collective-permute-start | bytes 24584 | tf_op jit(solution)/shard_map/while/body/eval_jaxpr/ppermute | solution.py:26
  (50 other events, 278.7 us)
where the time goes:
time: 678 us; the launch traced here: 666 us
  starting transfers between devices  339 us (50%)
  waiting for transfers between devices  298 us (44%)
  other arithmetic  16.5 us (2%)
  local copies, waits for them, and re-layouts  9.75 us (1%)
    ppermute x32, waiting for transfers between devices, from_behind(): lax.ppermute(value, axis, [(source, source + steps) for source in range(f...  260 us
    ppermute x39, starting transfers between devices, with_halo(): before = lax.ppermute(last, axis, up)  179 us
    ppermute x32, starting transfers between devices, from_behind(): lax.ppermute(value, axis, [(source, source + steps) for source in range(f...  82.8 us
    ppermute x39, starting transfers between devices, with_halo(): after = lax.ppermute(first, axis, down)  77.3 us
    ppermute x39, waiting for transfers between devices, with_halo(): after = lax.ppermute(first, axis, down)  19.2 us
    ppermute x39, waiting for transfers between devices, with_halo(): before = lax.ppermute(last, axis, up)  19.2 us
  transfers between devices with their start and end apart: 110, of which 71 were waited for; matrix products, arithmetic and copies ran while one was open for 1% of the time, Pallas kernels for 0%

commit v1 on v0

v1 whole, which is shorter than its diff:
```python
import functools

import jax
import jax.numpy as jnp
from jax import lax
from jax.experimental import pallas as pl
from jax.experimental.pallas import tpu as pltpu
from jax.sharding import PartitionSpec as P

MESH = pl.DeviceIdType.MESH
ADVECT = 0.01
LANES = 128
STEPS = 8
SPAN = 8
ROWS = 32
HALO = STEPS + SPAN
TALL = ROWS + 2 * HALO
TRIM = TALL - 2 * STEPS
SIDE = 32
OWN = LANES - 2 * SIDE


def shifted(u):
    rows = u.shape[0]
    up_left = pltpu.roll(u, 1, 0) + pltpu.roll(u, 1, 1)
    down_right = pltpu.roll(u, rows - 1, 0) + pltpu.roll(u, LANES - 1, 1)
    return up_left, down_right


def lanes_of(shape):
    return lax.broadcasted_iota(jnp.int32, shape, 1)


def kernel(
    nt, nz, initial_hbm, guess_hbm, kappa_hbm, forcing_hbm, amp_ref, out_ref,
    guess, pairs, windows, params, states, coarse, fine, amps, residual, error, edges, packed, arrived,
    load_sem, pair_sem, win_send, win_recv, par_send, par_recv, z_send, z_recv, edge_send, edge_recv, back_send, back_recv,
):
    tm, z = lax.axis_index("tm"), lax.axis_index("space")
    tiles = guess.shape[1] // LANES
    has_up, has_down = z > 0, z < nz - 1
    before, after = lax.rem(tm + nt - 1, nt), lax.rem(tm + 1, nt)

    barrier = pltpu.get_barrier_semaphore()

    def greet(t, where):
        pl.semaphore_signal(barrier, inc=1, device_id=(t, where), device_id_type=MESH)

    def greet_plane(k, carry):
        greet(lax.rem(tm + k, nt), z)
        return carry

    lax.fori_loop(1, nt, greet_plane, 0)

    @pl.when(has_up)
    def _():
        for t in (tm, before, after):
            greet(t, z - 1)

    @pl.when(has_down)
    def _():
        for t in (tm, before, after):
            greet(t, z + 1)

    load_guess = pltpu.make_async_copy(guess_hbm.at[0], guess, load_sem)
    load_guess.start()
    first = lax.rem(lax.div(tm + nt - 1, 2), tiles)
    second = lax.rem(first + 1, tiles)
    loads = []
    for i, ref in enumerate((initial_hbm, kappa_hbm, forcing_hbm)):
        for k, tile in enumerate((first, second)):
            columns = pl.ds(pl.multiple_of(tile * LANES, LANES), LANES)
            loads.append(pltpu.make_async_copy(ref.at[:, columns], pairs.at[i, k], pair_sem.at[i, k]))
    for load in loads:
        load.start()

    @pl.when(jnp.logical_not(has_up))
    def _():
        params[:, :HALO, :] = jnp.zeros((3, HALO, LANES), jnp.float32)
        states[:, :HALO, :] = jnp.zeros((nt + 1, HALO, LANES), jnp.float32)

    @pl.when(jnp.logical_not(has_down))
    def _():
        params[:, HALO + ROWS :, :] = jnp.zeros((3, HALO, LANES), jnp.float32)
        states[:, HALO + ROWS :, :] = jnp.zeros((nt + 1, HALO, LANES), jnp.float32)

    row_index = lax.broadcasted_iota(jnp.int32, (ROWS, LANES), 0)
    lane = lanes_of((ROWS, LANES))
    marks = jnp.zeros((ROWS, LANES), jnp.float32)
    for k in range(STEPS):
        marks = jnp.where(row_index == k, amp_ref[k], marks)
    marked = (lane == 0) & (row_index < STEPS)

    load_guess.wait()

    def tile_of(i):
        return guess[:, pl.ds(pl.multiple_of(i * LANES, LANES), LANES)]

    def cut(i, carry):
        low, mid, high = (tile_of(lax.rem(i + d, tiles)) for d in (tiles - 1, 0, 1))
        even = jnp.where(lane < SIDE, pltpu.roll(low, SIDE, 1), pltpu.roll(mid, SIDE, 1))
        odd = jnp.where(lane < LANES - SIDE, pltpu.roll(mid, LANES - SIDE, 1), pltpu.roll(high, LANES - SIDE, 1))
        windows[2 * i] = jnp.where(marked, marks, even)
        windows[2 * i + 1] = jnp.where(marked, marks, odd)
        return carry

    lax.fori_loop(0, tiles, cut, 0)
    pl.semaphore_wait(barrier, nt - 1 + 3 * has_up.astype(jnp.int32) + 3 * has_down.astype(jnp.int32))

    body = pl.ds(HALO, ROWS)

    def window_copy(source, target):
        return pltpu.make_async_remote_copy(
            windows.at[target], states.at[source + 1, body], win_send.at[target], win_recv.at[source],
            device_id=(target, z), device_id_type=MESH,
        )

    def send_window(k, carry):
        window_copy(tm, lax.rem(tm + k, nt)).start()
        return carry

    lax.fori_loop(1, nt, send_window, 0)
    states[tm + 1, HALO : HALO + ROWS, :] = windows[tm]

    for load in loads:
        load.wait()
    shift = jnp.where(lax.rem(tm, 2) == 0, SIDE, LANES - SIDE)
    for i in range(3):
        low, high = pltpu.roll(pairs[i, 0], shift, 1), pltpu.roll(pairs[i, 1], shift, 1)
        value = jnp.where(lane < shift, low, high)
        if i == 0:
            states[0, HALO : HALO + ROWS, :] = value
        params[i, HALO : HALO + ROWS, :] = value

    def params_up():
        return pltpu.make_async_remote_copy(
            params.at[:, pl.ds(HALO, HALO)], params.at[:, pl.ds(HALO + ROWS, HALO)], par_send.at[0], par_recv.at[0],
            device_id=(tm, z - 1), device_id_type=MESH,
        )

    def params_down():
        return pltpu.make_async_remote_copy(
            params.at[:, pl.ds(ROWS, HALO)], params.at[:, pl.ds(0, HALO)], par_send.at[1], par_recv.at[1],
            device_id=(tm, z + 1), device_id_type=MESH,
        )

    def state_up(t):
        return pltpu.make_async_remote_copy(
            states.at[t, pl.ds(HALO, HALO)], states.at[t, pl.ds(HALO + ROWS, HALO)], z_send.at[0, t], z_recv.at[0, t],
            device_id=(tm, z - 1), device_id_type=MESH,
        )

    def state_down(t):
        return pltpu.make_async_remote_copy(
            states.at[t, pl.ds(ROWS, HALO)], states.at[t, pl.ds(0, HALO)], z_send.at[1, t], z_recv.at[1, t],
            device_id=(tm, z + 1), device_id_type=MESH,
        )

    @pl.when(has_up)
    def _():
        params_up().start()

    @pl.when(has_down)
    def _():
        params_down().start()

    def forward(t, carry):
        @pl.when(t != tm)
        def _():
            window_copy(t, tm).wait_recv()

        @pl.when(has_up)
        def _():
            state_up(t + 1).start()

        @pl.when(has_down)
        def _():
            state_down(t + 1).start()

        return carry

    lax.fori_loop(0, nt, forward, 0)

    @pl.when(has_down)
    def _():
        params_up().wait_recv()

    @pl.when(has_up)
    def _():
        params_down().wait_recv()

    states[0, :HALO, :] = params[0, :HALO, :]
    states[0, HALO + ROWS :, :] = params[0, HALO + ROWS :, :]
    rows = lax.broadcasted_iota(jnp.int32, (TALL, LANES), 0)
    inside = ((rows >= HALO) | has_up) & ((rows < HALO + ROWS) | has_down)
    kappa = params[1]
    for ref, factor in ((fine, 1.0), (coarse, float(STEPS))):
        trim = slice(0, TALL) if ref is fine else slice(STEPS, STEPS + TRIM)
        ref[0] = jnp.where(inside, 1.0 - factor * (4.0 * kappa + 2.0 * ADVECT), 0.0)[trim]
        ref[1] = jnp.where(inside, factor * (kappa + ADVECT), 0.0)[trim]
        ref[2] = jnp.where(inside, factor * kappa, 0.0)[trim]
    fine[3] = jnp.where(inside, params[2], 0.0)

    def relax(t, carry):
        @pl.when(has_down)
        def _():
            state_up(t + 1).wait_recv()

        @pl.when(has_up)
        def _():
            state_down(t + 1).wait_recv()

        amps[...] = jnp.broadcast_to(states[t + 1, HALO : HALO + STEPS, 0:1], (STEPS, LANES))
        u = states[t]
        for k in range(STEPS):
            up_left, down_right = shifted(u)
            u = fine[0] * u + fine[1] * up_left + fine[2] * down_right + amps[k : k + 1, :] * fine[3]
        residual[t] = u[STEPS : STEPS + TRIM] - states[t + 1, STEPS : STEPS + TRIM, :]
        return carry

    def back_copy(source, target):
        return pltpu.make_async_remote_copy(
            packed.at[target], arrived.at[source], back_send.at[target], back_recv.at[source],
            device_id=(target, z), device_id_type=MESH,
        )

    half = ROWS // 2
    lane_half = lanes_of((half, LANES))

    def sweep(t, e):
        up_left, down_right = shifted(e)
        e = coarse[0] * e + coarse[1] * up_left + coarse[2] * down_right + residual[t]
        top, bottom = e[SPAN : SPAN + half], e[SPAN + half : SPAN + ROWS]
        both = jnp.where(lane_half < OWN, pltpu.roll(top, LANES - SIDE, 1), pltpu.roll(bottom, SIDE, 1))

        @pl.when(t == tm)
        def _():
            arrived[t] = both

        @pl.when(t != tm)
        def _():
            packed[t] = both
            back_copy(tm, t).start()

        return e

    edge_rows = {-1: (pl.ds(SPAN, SPAN), pl.ds(SPAN + ROWS, SPAN)), 1: (pl.ds(ROWS, SPAN), pl.ds(0, SPAN)), 0: (pl.ds(SPAN, ROWS), pl.ds(SPAN, ROWS))}

    def edge_copies(s):
        for dz in (-1, 0, 1):
            for slot, target in ((2, before), (1, tm), (0, after)):
                if dz == 0 and slot == 1:
                    continue
                here, there = edge_rows[dz]
                copy = pltpu.make_async_remote_copy(
                    error.at[s, here], edges.at[s, slot, there], edge_send.at[s, slot, dz + 1], edge_recv.at[s, slot, dz + 1],
                    device_id=(target, z + dz), device_id_type=MESH,
                )
                yield dz, copy

    def when_dz(dz, send, do):
        if dz == 0:
            do()
        else:
            up = (dz == -1) == send
            pl.when(has_up if up else has_down)(do)

    stages = nt // SPAN
    lane_trim = lanes_of((TRIM, LANES))
    row_trim = lax.broadcasted_iota(jnp.int32, (TRIM, LANES), 0)
    centre = (row_trim >= SPAN) & (row_trim < SPAN + ROWS)

    e = jnp.zeros((TRIM, LANES), jnp.float32)
    for s in range(stages):
        lax.fori_loop(s * SPAN, (s + 1) * SPAN, relax, 0)
        if s > 0:
            for dz, copy in edge_copies(s - 1):
                when_dz(dz, False, copy.wait_recv)
            left = pltpu.roll(edges[s - 1, 0], OWN, 1)
            right = pltpu.roll(edges[s - 1, 2], OWN, 1)
            own = jnp.where(centre, error[s - 1], edges[s - 1, 1])
            e = jnp.where(lane_trim < SIDE, left, jnp.where(lane_trim >= LANES - SIDE, right, own))
        e = lax.fori_loop(s * SPAN, (s + 1) * SPAN, sweep, e)
        if s < stages - 1:
            error[s] = e
            for slot in range(3):
                @pl.when(jnp.logical_not(has_up))
                def _():
                    edges[s, slot, :SPAN, :] = jnp.zeros((SPAN, LANES), jnp.float32)

                @pl.when(jnp.logical_not(has_down))
                def _():
                    edges[s, slot, SPAN + ROWS :, :] = jnp.zeros((SPAN, LANES), jnp.float32)

            for dz, copy in edge_copies(s):
                when_dz(dz, True, copy.start)

    def collect(k, carry):
        back_copy(lax.rem(tm + k, nt), tm).wait_recv()
        return carry

    lax.fori_loop(1, nt, collect, 0)

    def join(i, carry):
        first, second = arrived[2 * i], arrived[2 * i + 1]
        columns = pl.ds(pl.multiple_of(i * LANES, LANES), LANES)
        top = jnp.where(lane_half < OWN, first, pltpu.roll(second, OWN, 1))
        bottom = jnp.where(lane_half < OWN, pltpu.roll(first, OWN, 1), second)
        out_ref[0, :half, columns] = guess[:half, columns] + top
        out_ref[0, half:, columns] = guess[half:, columns] + bottom
        return carry

    lax.fori_loop(0, tiles, join, 0)

    def sent(k, carry):
        t = lax.rem(tm + k, nt)
        window_copy(tm, t).wait_send()
        back_copy(tm, t).wait_send()
        return carry

    lax.fori_loop(1, nt, sent, 0)

    @pl.when(has_up)
    def _():
        params_up().wait_send()
        lax.fori_loop(1, nt + 1, lambda t, carry: (state_up(t).wait_send(), carry)[1], 0)

    @pl.when(has_down)
    def _():
        params_down().wait_send()
        lax.fori_loop(1, nt + 1, lambda t, carry: (state_down(t).wait_send(), carry)[1], 0)

    for s in range(stages - 1):
        for dz, copy in edge_copies(s):
            when_dz(dz, True, copy.wait_send)


def per_device(initial_state, guesses, diffusivity, forcing_field, amplitudes):
    nt, nz = lax.axis_size("tm"), lax.axis_size("space")
    rows, cols = initial_state.shape
    stages = nt // SPAN
    dma = pltpu.SemaphoreType.DMA
    vmem = functools.partial(pltpu.VMEM, dtype=jnp.float32)
    hbm = pl.BlockSpec(memory_space=pl.ANY)
    return pl.pallas_call(
        functools.partial(kernel, nt, nz),
        out_shape=jax.ShapeDtypeStruct((1, rows, cols), jnp.float32),
        in_specs=[hbm] * 4 + [pl.BlockSpec(memory_space=pltpu.SMEM)],
        out_specs=pl.BlockSpec(memory_space=pltpu.VMEM),
        scratch_shapes=[
            vmem((rows, cols)),
            vmem((3, 2, rows, LANES)),
            vmem((nt, rows, LANES)),
            vmem((3, TALL, LANES)),
            vmem((nt + 1, TALL, LANES)),
            vmem((3, TRIM, LANES)),
            vmem((4, TALL, LANES)),
            vmem((STEPS, LANES)),
            vmem((nt, TRIM, LANES)),
            vmem((stages - 1, TRIM, LANES)),
            vmem((stages - 1, 3, TRIM, LANES)),
            vmem((nt, rows // 2, LANES)),
            vmem((nt, rows // 2, LANES)),
            dma, dma((3, 2)), dma((nt,)), dma((nt,)), dma((2,)), dma((2,)), dma((2, nt + 1)), dma((2, nt + 1)),
            dma((stages - 1, 3, 3)), dma((stages - 1, 3, 3)), dma((nt,)), dma((nt,)),
        ],
        compiler_params=pltpu.CompilerParams(collective_id=0, has_side_effects=True, vmem_limit_bytes=32 * 2**20),
    )(initial_state, guesses, diffusivity, forcing_field, amplitudes)


def solution(mesh):
    placed = (P("space", None), P("tm", "space", None), P("space", None), P("space", None), P("tm"))
    return jax.shard_map(
        per_device, mesh=mesh, in_specs=placed, out_specs=P("tm", "space", None), check_vma=False
    )
```

time: 678 us -> 57.8 us (0.09); the launches traced: 666 us -> 56.7 us
  starting transfers between devices: 339 us -> 0 us
  waiting for transfers between devices: 298 us -> 0 us
  Pallas kernels: 0 us -> 51.5 us
  other arithmetic: 16.5 us -> 0 us
    ppermute x110 -> x0, starting transfers between devices: 339 us -> none  [the longest x39 179 us: with_halo(): before = lax.ppermute(last, axis, up)]
    ppermute x110 -> x0, waiting for transfers between devices: 298 us -> none  [the longest x32 260 us: from_behind(): lax.ppermute(value, axis, [(source, source + steps) for source in range(f...]
    pallas_call x0 -> x1, Pallas kernels: none -> 51.5 us  [per_device(): pl.pallas_call(functools.partial(kernel, nt, nz), out_shape=jax.ShapeDtyp...]
    select_n x33 -> x0, other arithmetic: 9.92 us -> none  [the longest x31 9.1 us: relay_turn(): return jnp.where(j == tm_index, update, error_field)]
    slice x118 -> x0, local copies, waits for them, and re-layouts: 9.09 us -> none  [the longest x78 7.9 us: advance(): left_cols = jnp.roll(center, 1, axis=-1)]
  transfers between devices with their start and end apart: 110 -> 0, of which waited for: 71 -> 0; matrix products, arithmetic and copies ran while one was open for 1% -> 0% of each run, Pallas kernels for 0% -> 0%
where the time goes in v1:
time: 57.8 us; the launch traced here: 56.7 us
  Pallas kernels  51.5 us (89%)
  local copies, waits for them, and re-layouts  5.16 us (9%)
    pallas_call x1, Pallas kernels, per_device(): pl.pallas_call(functools.partial(kernel, nt, nz), out_shape=jax.ShapeDtyp...  51.5 us
    unnamed x11, local copies, waits for them, and re-layouts  5.16 us

profile of v1, /device:TPU:89, one launch (start us, length us, event | category | flops | bytes accessed | tf_op | source)
XLA Modules:
  0.0 56.7 jit_solution(10812458358696148004)
XLA Ops:
  0.0 0.0 copy-start
  0.0 0.9 %copy-done = f32[32,2048]{1,0:T(8,128)S(1)} copy-done((f32[32,2048]{1,0:T(8,128)S(1)}, f32[32,2048]{1,0:T(8,128)}, u32[]{:S(2)}) %copy-start) | copy-done | bytes 262168
  1.0 0.0 copy-start.1
  1.0 0.9 %copy-done.1 = f32[1,32,2048]{2,1,0:T(8,128)S(1)} copy-done((f32[1,32,2048]{2,1,0:T(8,128)S(1)}, f32[1,32,2048]{2,1,0:T(8,128)}, u32[]{:S(2)}) %copy-start.1) | copy-done | bytes 262168
  1.9 0.0 copy-start.2
  1.9 0.9 %copy-done.2 = f32[32,2048]{1,0:T(8,128)S(1)} copy-done((f32[32,2048]{1,0:T(8,128)S(1)}, f32[32,2048]{1,0:T(8,128)}, u32[]{:S(2)}) %copy-start.2) | copy-done | bytes 262168
  2.9 0.0 copy-start.3
  2.9 0.9 %copy-done.3 = f32[32,2048]{1,0:T(8,128)S(1)} copy-done((f32[32,2048]{1,0:T(8,128)S(1)}, f32[32,2048]{1,0:T(8,128)}, u32[]{:S(2)}) %copy-start.3) | copy-done | bytes 262168
  3.8 0.0 copy-start.4
  3.8 0.7 %copy-done.4 = f32[8]{0:T(128)S(1)} copy-done((f32[8]{0:T(128)S(1)}, f32[8]{0:T(128)}, u32[]{:S(2)}) %copy-start.4) | copy-done | bytes 56
  4.5 51.5 %shard_map.55 = f32[1,32,2048]{2,1,0:T(8,128)S(1)} custom-call(f32[32,2048]{1,0:T(8,128)S(1)} %copy-done, f32[1,32,2048]{2,1,0:T(8,128)S(1)} %copy-done.1, f32[32,2048]{1,0:T(8,128)S(1)} %copy-done.2, f32[32,2048]{1,0:T(8,128)S(1)} %copy-done.3, f32[8]{0:T(128)S(1)} %copy-done.4), custom_call_target="tpu_custom_call" | custom-call | tf_op jit(solution)/shard_map/pallas_call | solution.py:345
  56.0 0.7 %copy.7 = f32[1,32,2048]{2,1,0:T(8,128)} copy(f32[1,32,2048]{2,1,0:T(8,128)S(1)} %shard_map.55) | data formatting | bytes 524288
Async XLA Ops:
  0.0 0.9 %copy-start = (f32[32,2048]{1,0:T(8,128)S(1)}, f32[32,2048]{1,0:T(8,128)}, u32[]{:S(2)}) copy-start(f32[32,2048]{1,0:T(8,128)} %initial_hbm.1) | copy-start | bytes 786436
  1.0 0.9 %copy-start.1 = (f32[1,32,2048]{2,1,0:T(8,128)S(1)}, f32[1,32,2048]{2,1,0:T(8,128)}, u32[]{:S(2)}) copy-start(f32[1,32,2048]{2,1,0:T(8,128)} %guess_hbm.1) | copy-start | bytes 786436
  1.9 0.9 %copy-start.2 = (f32[32,2048]{1,0:T(8,128)S(1)}, f32[32,2048]{1,0:T(8,128)}, u32[]{:S(2)}) copy-start(f32[32,2048]{1,0:T(8,128)} %kappa_hbm.1) | copy-start | bytes 786436
  2.9 0.9 %copy-start.3 = (f32[32,2048]{1,0:T(8,128)S(1)}, f32[32,2048]{1,0:T(8,128)}, u32[]{:S(2)}) copy-start(f32[32,2048]{1,0:T(8,128)} %forcing_hbm.1) | copy-start | bytes 786436
  3.8 0.7 %copy-start.4 = (f32[8]{0:T(128)S(1)}, f32[8]{0:T(128)}, u32[]{:S(2)}) copy-start(f32[8]{0:T(128)} %amp_ref.1) | copy-start | bytes 100

commit v2 on v1

v2 whole, which is shorter than its diff:
```python
import functools

import jax
import jax.numpy as jnp
from jax import lax
from jax.experimental import pallas as pl
from jax.experimental.pallas import tpu as pltpu
from jax.sharding import PartitionSpec as P

MESH = pl.DeviceIdType.MESH
ADVECT = 0.01
LANES = 128
STEPS = 8
SPAN = 16
ROWS = 32
HALO = STEPS + SPAN
TALL = ROWS + 2 * HALO
TRIM = TALL - 2 * STEPS
GROUP = 8
BLOCK = 6
SIDE = 32
OWN = LANES - 2 * SIDE


def spans(slabs):
    found = []
    for first in range(0, slabs, SPAN):
        for place in range(SPAN):
            width = (STEPS + SPAN - 1 - place + 7) // 8 * 8
            if found and found[-1][2] == width and place:
                found[-1][1] = first + place + 1
            else:
                found.append([first + place, first + place + 1, width])
    return found


def lanes_of(shape):
    return lax.broadcasted_iota(jnp.int32, shape, 1)


def kernel(
    nt, nz, initial_hbm, guess_hbm, kappa_hbm, forcing_hbm, amp_hbm, out_ref,
    amp_ref, guess, pairs, windows, params, states, coarse, fine, amps, here, there, residual, error, edges, packed, arrived,
    amp_sem, load_sem, pair_sem, win_send, win_recv, par_send, par_recv, z_send, z_recv, edge_send, edge_recv, back_send, back_recv,
):
    tm, z = lax.axis_index("tm"), lax.axis_index("space")
    tiles = guess.shape[1] // LANES
    widths = spans(nt)
    has_up, has_down = z > 0, z < nz - 1
    before, after = lax.rem(tm + nt - 1, nt), lax.rem(tm + 1, nt)

    barrier = pltpu.get_barrier_semaphore()

    def greet(t, where):
        pl.semaphore_signal(barrier, inc=1, device_id=(t, where), device_id_type=MESH)

    def greet_plane(k, carry):
        greet(lax.rem(tm + k, nt), z)
        return carry

    lax.fori_loop(1, nt, greet_plane, 0)

    @pl.when(has_up)
    def _():
        for t in (tm, before, after):
            greet(t, z - 1)

    @pl.when(has_down)
    def _():
        for t in (tm, before, after):
            greet(t, z + 1)

    load_guess = pltpu.make_async_copy(guess_hbm.at[0], guess, load_sem)
    load_guess.start()
    load_amps = pltpu.make_async_copy(amp_hbm, amp_ref, amp_sem)
    load_amps.start()
    first = lax.rem(lax.div(tm + nt - 1, 2), tiles)
    second = lax.rem(first + 1, tiles)
    loads = []
    for i, ref in enumerate((initial_hbm, kappa_hbm, forcing_hbm)):
        for k, tile in enumerate((first, second)):
            columns = pl.ds(pl.multiple_of(tile * LANES, LANES), LANES)
            loads.append(pltpu.make_async_copy(ref.at[:, columns], pairs.at[i, k], pair_sem.at[i, k]))
    for load in loads:
        load.start()

    def state_rows(t, first, count):
        return pl.ds(pl.multiple_of(t * TALL + first, 8), count)

    def clear(first, t, carry):
        states[state_rows(t, first, HALO), :] = jnp.zeros((HALO, LANES), jnp.float32)
        return carry

    @pl.when(jnp.logical_not(has_up))
    def _():
        params[:, :HALO, :] = jnp.zeros((3, HALO, LANES), jnp.float32)
        lax.fori_loop(0, nt + 1, functools.partial(clear, 0), 0)

    @pl.when(jnp.logical_not(has_down))
    def _():
        params[:, HALO + ROWS :, :] = jnp.zeros((3, HALO, LANES), jnp.float32)
        lax.fori_loop(0, nt + 1, functools.partial(clear, HALO + ROWS), 0)

    row_index = lax.broadcasted_iota(jnp.int32, (ROWS, LANES), 0)
    lane = lanes_of((ROWS, LANES))
    marks = jnp.zeros((ROWS, LANES), jnp.float32)
    load_amps.wait()
    for k in range(STEPS):
        marks = jnp.where(row_index == k, amp_ref[k], marks)
    marked = (lane == 0) & (row_index < STEPS)

    load_guess.wait()

    def tile_of(i):
        return guess[:, pl.ds(pl.multiple_of(i * LANES, LANES), LANES)]

    def cut(i, carry):
        low, mid, high = (tile_of(lax.rem(i + d, tiles)) for d in (tiles - 1, 0, 1))
        even = jnp.where(lane < SIDE, pltpu.roll(low, SIDE, 1), pltpu.roll(mid, SIDE, 1))
        odd = jnp.where(lane < LANES - SIDE, pltpu.roll(mid, LANES - SIDE, 1), pltpu.roll(high, LANES - SIDE, 1))
        windows[2 * i] = jnp.where(marked, marks, even)
        windows[2 * i + 1] = jnp.where(marked, marks, odd)
        return carry

    lax.fori_loop(0, tiles, cut, 0)
    pl.semaphore_wait(barrier, nt - 1 + 3 * has_up.astype(jnp.int32) + 3 * has_down.astype(jnp.int32))

    def window_copy(source, target):
        return pltpu.make_async_remote_copy(
            windows.at[target], states.at[state_rows(source + 1, HALO, ROWS)], win_send.at[target], win_recv.at[source],
            device_id=(target, z), device_id_type=MESH,
        )

    def send_window(k, carry):
        window_copy(tm, lax.rem(tm + k, nt)).start()
        return carry

    lax.fori_loop(1, nt, send_window, 0)
    states[state_rows(tm + 1, HALO, ROWS), :] = windows[tm]

    for load in loads:
        load.wait()
    shift = jnp.where(lax.rem(tm, 2) == 0, SIDE, LANES - SIDE)
    for i in range(3):
        low, high = pltpu.roll(pairs[i, 0], shift, 1), pltpu.roll(pairs[i, 1], shift, 1)
        value = jnp.where(lane < shift, low, high)
        if i == 0:
            states[HALO : HALO + ROWS, :] = value
        params[i, HALO : HALO + ROWS, :] = value

    def params_up():
        return pltpu.make_async_remote_copy(
            params.at[:, pl.ds(HALO, HALO)], params.at[:, pl.ds(HALO + ROWS, HALO)], par_send.at[0], par_recv.at[0],
            device_id=(tm, z - 1), device_id_type=MESH,
        )

    def params_down():
        return pltpu.make_async_remote_copy(
            params.at[:, pl.ds(ROWS, HALO)], params.at[:, pl.ds(0, HALO)], par_send.at[1], par_recv.at[1],
            device_id=(tm, z + 1), device_id_type=MESH,
        )

    def state_up(t, width):
        return pltpu.make_async_remote_copy(
            states.at[state_rows(t, HALO, width)], states.at[state_rows(t, HALO + ROWS, width)], z_send.at[0, t], z_recv.at[0, t],
            device_id=(tm, z - 1), device_id_type=MESH,
        )

    def state_down(t, width):
        return pltpu.make_async_remote_copy(
            states.at[state_rows(t, HALO + ROWS - width, width)], states.at[state_rows(t, HALO - width, width)], z_send.at[1, t], z_recv.at[1, t],
            device_id=(tm, z + 1), device_id_type=MESH,
        )

    @pl.when(has_up)
    def _():
        params_up().start()

    @pl.when(has_down)
    def _():
        params_down().start()

    def forward(width, t, carry):
        @pl.when(t != tm + 1)
        def _():
            window_copy(t - 1, tm).wait_recv()

        @pl.when(has_up)
        def _():
            state_up(t, width).start()

        @pl.when(has_down)
        def _():
            state_down(t, width).start()

        return carry

    for first, last, width in widths:
        lax.fori_loop(max(first, 1), last, functools.partial(forward, width), 0)

    @pl.when(tm != nt - 1)
    def _():
        window_copy(nt - 1, tm).wait_recv()

    @pl.when(has_down)
    def _():
        params_up().wait_recv()

    @pl.when(has_up)
    def _():
        params_down().wait_recv()

    states[:HALO, :] = params[0, :HALO, :]
    states[HALO + ROWS : TALL, :] = params[0, HALO + ROWS :, :]
    rows = lax.broadcasted_iota(jnp.int32, (TALL, LANES), 0)
    inside = ((rows >= HALO) | has_up) & ((rows < HALO + ROWS) | has_down)

    def factors(factor):
        kappa = params[1]
        centre = jnp.where(inside, 1.0 - factor * (4.0 * kappa + 2.0 * ADVECT), 0.0)
        return centre, jnp.where(inside, factor * (kappa + ADVECT), 0.0), jnp.where(inside, factor * kappa, 0.0)

    for i, value in enumerate(factors(1.0) + (jnp.where(inside, params[2], 0.0),)):
        fine[i] = jnp.broadcast_to(value[:, None, :], (TALL, GROUP, LANES))
    for i, value in enumerate(factors(float(STEPS))):
        coarse[i] = value[STEPS : STEPS + TRIM]

    def arrive(width, t, carry):
        @pl.when(has_down)
        def _():
            state_up(t, width).wait_recv()

        @pl.when(has_up)
        def _():
            state_down(t, width).wait_recv()

        return carry

    def slabs_at(t, r):
        return states[pl.ds(t * TALL + r, GROUP, stride=TALL), :]

    def fine_step(source, target, k, low, high):
        amp = amps[k]
        for r in range(low, high, BLOCK):
            end = min(r + BLOCK, high)
            u = source[r - 1 : end + 1]
            mid = u[1:-1]
            up_left = u[:-2] + pltpu.roll(mid, 1, 2)
            down_right = u[2:] + pltpu.roll(mid, LANES - 1, 2)
            target[r:end] = fine[0, r:end] * mid + fine[1, r:end] * up_left + fine[2, r:end] * down_right + amp * fine[3, r:end]

    def relax(group, edge):
        t = group * GROUP
        for k in range(STEPS):
            amps[k] = jnp.broadcast_to(slabs_at(t + 1, HALO + k)[:, 0:1], (GROUP, LANES))
        for r in range(edge, TALL - edge):
            here[r] = slabs_at(t, r)

        def two_steps(k, carry):
            fine_step(here, there, 2 * k, edge + 1, TALL - edge - 1)
            fine_step(there, here, 2 * k + 1, edge + 1, TALL - edge - 1)
            return carry

        lax.fori_loop(0, STEPS // 2, two_steps, 0)
        for r in range(edge + STEPS, TALL - edge - STEPS):
            residual[group, (r - STEPS) * GROUP : (r - STEPS + 1) * GROUP] = here[r] - slabs_at(t + 1, r)

    def back_copy(source, target):
        return pltpu.make_async_remote_copy(
            packed.at[target], arrived.at[source], back_send.at[target], back_recv.at[source],
            device_id=(target, z), device_id_type=MESH,
        )

    half = ROWS // 2
    lane_half = lanes_of((half, LANES))

    def coarse_at(i):
        return jnp.stack([coarse[i, pl.ds(b, 8, stride=8), :] for b in range(8)])

    def sweep(group, place, e):
        t = group * GROUP + place
        up = jnp.concatenate([pltpu.roll(e[-1:], 1, 1), e[:-1]], axis=0)
        down = jnp.concatenate([e[1:], pltpu.roll(e[:1], 7, 1)], axis=0)
        add = jnp.stack([residual[group, pl.ds(b * GROUP + place, 8, stride=8 * GROUP), :] for b in range(8)])
        e = coarse_at(0) * e + coarse_at(1) * (up + pltpu.roll(e, 1, 2)) + coarse_at(2) * (down + pltpu.roll(e, LANES - 1, 2)) + add
        for b in range(8):
            error[t, pl.ds(b, 8, stride=8), :] = e[b]
        both = jnp.where(
            lane_half < OWN,
            pltpu.roll(error[t, SPAN : SPAN + half, :], LANES - SIDE, 1),
            pltpu.roll(error[t, SPAN + half : SPAN + ROWS, :], SIDE, 1),
        )

        @pl.when(t == tm)
        def _():
            arrived[t] = both

        @pl.when(t != tm)
        def _():
            packed[t] = both
            back_copy(tm, t).start()

        return e

    edge_rows = {-1: (pl.ds(SPAN, SPAN), pl.ds(SPAN + ROWS, SPAN)), 1: (pl.ds(ROWS, SPAN), pl.ds(0, SPAN)), 0: (pl.ds(SPAN, ROWS), pl.ds(SPAN, ROWS))}

    def edge_copies(s):
        for dz in (-1, 0, 1):
            for slot, target in ((2, before), (1, tm), (0, after)):
                if dz == 0 and slot == 1:
                    continue
                rows_here, rows_there = edge_rows[dz]
                copy = pltpu.make_async_remote_copy(
                    error.at[(s + 1) * SPAN - 1, rows_here], edges.at[s, slot, rows_there], edge_send.at[s, slot, dz + 1], edge_recv.at[s, slot, dz + 1],
                    device_id=(target, z + dz), device_id_type=MESH,
                )
                yield dz, copy

    def when_dz(dz, send, do):
        if dz == 0:
            do()
        else:
            up = (dz == -1) == send
            pl.when(has_up if up else has_down)(do)

    stages = nt // SPAN
    lane_trim = lanes_of((TRIM, LANES))
    row_trim = lax.broadcasted_iota(jnp.int32, (TRIM, LANES), 0)
    centre = (row_trim >= SPAN) & (row_trim < SPAN + ROWS)

    e = jnp.zeros((8, 8, LANES), jnp.float32)
    for s in range(stages):
        for first, last, width in widths:
            first, last = max(first, s * SPAN + 1), min(last, (s + 1) * SPAN + 1)
            if first < last:
                lax.fori_loop(first, last, functools.partial(arrive, width), 0)
        for part in range(SPAN // GROUP):
            relax(s * (SPAN // GROUP) + part, part * GROUP)
        if s > 0:
            for dz, copy in edge_copies(s - 1):
                when_dz(dz, False, copy.wait_recv)
            left = pltpu.roll(edges[s - 1, 0], OWN, 1)
            right = pltpu.roll(edges[s - 1, 2], OWN, 1)
            own = jnp.where(centre, error[s * SPAN - 1], edges[s - 1, 1])
            edges[s - 1, 1] = jnp.where(lane_trim < SIDE, left, jnp.where(lane_trim >= LANES - SIDE, right, own))
            e = jnp.stack([edges[s - 1, 1, pl.ds(b, 8, stride=8), :] for b in range(8)])
        for part in range(SPAN // GROUP):
            e = lax.fori_loop(0, GROUP, functools.partial(sweep, s * (SPAN // GROUP) + part), e)
        if s < stages - 1:
            for slot in range(3):
                @pl.when(jnp.logical_not(has_up))
                def _():
                    edges[s, slot, :SPAN, :] = jnp.zeros((SPAN, LANES), jnp.float32)

                @pl.when(jnp.logical_not(has_down))
                def _():
                    edges[s, slot, SPAN + ROWS :, :] = jnp.zeros((SPAN, LANES), jnp.float32)

            for dz, copy in edge_copies(s):
                when_dz(dz, True, copy.start)

    def sent(k, carry):
        window_copy(tm, lax.rem(tm + k, nt)).wait_send()
        return carry

    lax.fori_loop(1, nt, sent, 0)

    def drain(copy, first, last, width):
        lax.fori_loop(max(first, 1), last, lambda t, carry: (copy(t, width).wait_send(), carry)[1], 0)

    @pl.when(has_up)
    def _():
        params_up().wait_send()
        for span in widths:
            drain(state_up, *span)

    @pl.when(has_down)
    def _():
        params_down().wait_send()
        for span in widths:
            drain(state_down, *span)

    for s in range(stages - 1):
        for dz, copy in edge_copies(s):
            when_dz(dz, True, copy.wait_send)

    def collect(k, carry):
        back_copy(lax.rem(tm + k, nt), tm).wait_recv()
        back_copy(tm, lax.rem(tm + k, nt)).wait_send()
        return carry

    lax.fori_loop(1, nt, collect, 0)

    def join(i, carry):
        first, second = arrived[2 * i], arrived[2 * i + 1]
        columns = pl.ds(pl.multiple_of(i * LANES, LANES), LANES)
        top = jnp.where(lane_half < OWN, first, pltpu.roll(second, OWN, 1))
        bottom = jnp.where(lane_half < OWN, pltpu.roll(first, OWN, 1), second)
        out_ref[0, :half, columns] = guess[:half, columns] + top
        out_ref[0, half:, columns] = guess[half:, columns] + bottom
        return carry

    lax.fori_loop(0, tiles, join, 0)


def per_device(initial_state, guesses, diffusivity, forcing_field, amplitudes):
    nt, nz = lax.axis_size("tm"), lax.axis_size("space")
    rows, cols = initial_state.shape
    stages = nt // SPAN
    dma = pltpu.SemaphoreType.DMA
    vmem = functools.partial(pltpu.VMEM, dtype=jnp.float32)
    hbm = pl.BlockSpec(memory_space=pl.ANY)
    return pl.pallas_call(
        functools.partial(kernel, nt, nz),
        out_shape=jax.ShapeDtypeStruct((1, rows, cols), jnp.float32),
        in_specs=[hbm] * 5,
        out_specs=pl.BlockSpec(memory_space=pltpu.VMEM),
        scratch_shapes=[
            pltpu.SMEM((STEPS,), jnp.float32),
            vmem((rows, cols)),
            vmem((3, 2, rows, LANES)),
            vmem((nt, rows, LANES)),
            vmem((3, TALL, LANES)),
            vmem(((nt + 1) * TALL, LANES)),
            vmem((3, TRIM, LANES)),
            vmem((4, TALL, GROUP, LANES)),
            vmem((STEPS, GROUP, LANES)),
            vmem((TALL, GROUP, LANES)),
            vmem((TALL, GROUP, LANES)),
            vmem((nt // GROUP, TRIM * GROUP, LANES)),
            vmem((nt, TRIM, LANES)),
            vmem((stages - 1, 3, TRIM, LANES)),
            vmem((nt, rows // 2, LANES)),
            vmem((nt, rows // 2, LANES)),
            dma, dma, dma((3, 2)), dma((nt,)), dma((nt,)), dma((2,)), dma((2,)), dma((2, nt + 1)), dma((2, nt + 1)),
            dma((stages - 1, 3, 3)), dma((stages - 1, 3, 3)), dma((nt,)), dma((nt,)),
        ],
        compiler_params=pltpu.CompilerParams(collective_id=0, has_side_effects=True, vmem_limit_bytes=60 * 2**20),
    )(initial_state, guesses, diffusivity, forcing_field, amplitudes)


def solution(mesh):
    placed = (P("space", None), P("tm", "space", None), P("space", None), P("space", None), P("tm"))
    return jax.shard_map(
        per_device, mesh=mesh, in_specs=placed, out_specs=P("tm", "space", None), check_vma=False
    )
```

time: 57.8 us -> 44.4 us (0.77)
  the two profiles are of different devices: /device:TPU:89 before, /device:TPU:95 now
where the time goes in v2:
time: 44.4 us; the launch traced here: 44.3 us
  Pallas kernels  42.6 us (96%)
  local copies, waits for them, and re-layouts  1.67 us (4%)
    pallas_call x1, Pallas kernels, per_device(): pl.pallas_call(functools.partial(kernel, nt, nz), out_shape=jax.ShapeDtyp...  42.6 us
    unnamed x1, local copies, waits for them, and re-layouts  1.67 us

profile of v2, /device:TPU:95, one launch (start us, length us, event | category | flops | bytes accessed | tf_op | source)
XLA Modules:
  0.0 44.3 jit_solution(7554346427743947418)
XLA Ops:
  0.0 42.6 %shard_map.55 = f32[1,32,2048]{2,1,0:T(8,128)} custom-call(f32[32,2048]{1,0:T(8,128)} %initial_hbm.1, f32[1,32,2048]{2,1,0:T(8,128)} %guess_hbm.1, f32[32,2048]{1,0:T(8,128)} %kappa_hbm.1, f32[32,2048]{1,0:T(8,128)} %forcing_hbm.1, f32[8]{0:T(128)} %amp_hbm.1), custom_call_target="tpu_custom_call" | custom-call | tf_op jit(solution)/shard_map/pallas_call | solution.py:413
  42.6 1.7 %copy.7 = f32[1,32,2048]{2,1,0:T(8,128)} copy(f32[1,32,2048]{2,1,0:T(8,128)} %shard_map.55) | data formatting | bytes 524288

commit v3 on v2

--- a/solution.py
+++ b/solution.py
@@ -22,15 +22,17 @@
 OWN = LANES - 2 * SIDE
 
 
-def spans(slabs):
+def width_of(place):
+    return (STEPS + SPAN - 1 - place + 7) // 8 * 8
+
+
+def spans():
     found = []
-    for first in range(0, slabs, SPAN):
-        for place in range(SPAN):
-            width = (STEPS + SPAN - 1 - place + 7) // 8 * 8
-            if found and found[-1][2] == width and place:
-                found[-1][1] = first + place + 1
-            else:
-                found.append([first + place, first + place + 1, width])
+    for place in range(SPAN):
+        if found and found[-1][2] == width_of(place):
+            found[-1][1] = place + 1
+        else:
+            found.append([place, place + 1, width_of(place)])
     return found
 
 
@@ -40,12 +42,12 @@
 
 def kernel(
     nt, nz, initial_hbm, guess_hbm, kappa_hbm, forcing_hbm, amp_hbm, out_ref,
-    amp_ref, guess, pairs, windows, params, states, coarse, fine, amps, here, there, residual, error, edges, packed, arrived,
+    amp_ref, guess, pairs, windows, params, states, coarse, fine, amps, here, there, residual, error, edges, starts, packed, arrived,
     amp_sem, load_sem, pair_sem, win_send, win_recv, par_send, par_recv, z_send, z_recv, edge_send, edge_recv, back_send, back_recv,
 ):
     tm, z = lax.axis_index("tm"), lax.axis_index("space")
     tiles = guess.shape[1] // LANES
-    widths = spans(nt)
+    widths = spans()
     has_up, has_down = z > 0, z < nz - 1
     before, after = lax.rem(tm + nt - 1, nt), lax.rem(tm + 1, nt)
 
@@ -101,6 +103,14 @@
         params[:, HALO + ROWS :, :] = jnp.zeros((3, HALO, LANES), jnp.float32)
         lax.fori_loop(0, nt + 1, functools.partial(clear, HALO + ROWS), 0)
 
+    @pl.when(jnp.logical_not(has_up))
+    def _():
+        edges[:, :, :SPAN, :] = jnp.zeros((nt // SPAN - 1, 3, SPAN, LANES), jnp.float32)
+
+    @pl.when(jnp.logical_not(has_down))
+    def _():
+        edges[:, :, SPAN + ROWS :, :] = jnp.zeros((nt // SPAN - 1, 3, SPAN, LANES), jnp.float32)
+
     row_index = lax.broadcasted_iota(jnp.int32, (ROWS, LANES), 0)
     lane = lanes_of((ROWS, LANES))
     marks = jnp.zeros((ROWS, LANES), jnp.float32)
@@ -195,8 +205,12 @@
 
         return carry
 
-    for first, last, width in widths:
-        lax.fori_loop(max(first, 1), last, functools.partial(forward, width), 0)
+    def forward_stage(s, carry):
+        for first, last, width in widths:
+            lax.fori_loop(jnp.maximum(s * SPAN + first, 1), s * SPAN + last, functools.partial(forward, width), 0)
+        return carry
+
+    lax.fori_loop(0, nt // SPAN, forward_stage, 0)
 
     @pl.when(tm != nt - 1)
     def _():
@@ -212,18 +226,24 @@
 
     states[:HALO, :] = params[0, :HALO, :]
     states[HALO + ROWS : TALL, :] = params[0, HALO + ROWS :, :]
-    rows = lax.broadcasted_iota(jnp.int32, (TALL, LANES), 0)
-    inside = ((rows >= HALO) | has_up) & ((rows < HALO + ROWS) | has_down)
-
-    def factors(factor):
-        kappa = params[1]
-        centre = jnp.where(inside, 1.0 - factor * (4.0 * kappa + 2.0 * ADVECT), 0.0)
-        return centre, jnp.where(inside, factor * (kappa + ADVECT), 0.0), jnp.where(inside, factor * kappa, 0.0)
-
-    for i, value in enumerate(factors(1.0) + (jnp.where(inside, params[2], 0.0),)):
-        fine[i] = jnp.broadcast_to(value[:, None, :], (TALL, GROUP, LANES))
-    for i, value in enumerate(factors(float(STEPS))):
-        coarse[i] = value[STEPS : STEPS + TRIM]
+
+    def factors(i, carry):
+        rows = pl.ds(pl.multiple_of(i * GROUP, GROUP), GROUP)
+        row = i * GROUP + lax.broadcasted_iota(jnp.int32, (GROUP, LANES), 0)
+        inside = ((row >= HALO) | has_up) & ((row < HALO + ROWS) | has_down)
+        kappa = params[1, rows, :]
+        for ref, factor in ((fine, 1.0), (coarse, float(STEPS))):
+            for k, value in enumerate((1.0 - factor * (4.0 * kappa + 2.0 * ADVECT), factor * (kappa + ADVECT), factor * kappa)):
+                value = jnp.where(inside, value, 0.0)
+                if ref is fine:
+                    fine[k, rows] = jnp.broadcast_to(value[:, None, :], (GROUP, GROUP, LANES))
+                else:
+                    coarse[k, rows, :] = value
+        forcing = jnp.where(inside, params[2, rows, :], 0.0)
+        fine[3, rows] = jnp.broadcast_to(forcing[:, None, :], (GROUP, GROUP, LANES))
+        return carry
+
+    lax.fori_loop(0, TALL // GROUP, factors, 0)
 
     def arrive(width, t, carry):
         @pl.when(has_down)
@@ -239,31 +259,60 @@
     def slabs_at(t, r):
         return states[pl.ds(t * TALL + r, GROUP, stride=TALL), :]
 
-    def fine_step(source, target, k, low, high):
+    def fine_step(source, target, k):
         amp = amps[k]
-        for r in range(low, high, BLOCK):
-            end = min(r + BLOCK, high)
+        for r in range(1, TALL - 1, BLOCK):
+            end = min(r + BLOCK, TALL - 1)
             u = source[r - 1 : end + 1]
             mid = u[1:-1]
             up_left = u[:-2] + pltpu.roll(mid, 1, 2)
             down_right = u[2:] + pltpu.roll(mid, LANES - 1, 2)
             target[r:end] = fine[0, r:end] * mid + fine[1, r:end] * up_left + fine[2, r:end] * down_right + amp * fine[3, r:end]
 
-    def relax(group, edge):
+    def arrivals(s, parity):
+        first = parity * GROUP + 1
+        for place in range(first, first + GROUP):
+            width = width_of(place % SPAN)
+            if place > first and width == width_of((place - 1) % SPAN):
+                continue
+            last = place
+            while last < first + GROUP and width_of(last % SPAN) == width:
+                last += 1
+            lax.fori_loop(s * SPAN + place, jnp.minimum(s * SPAN + last, nt), functools.partial(arrive, width), 0)
+
+    def relax(group, carry):
         t = group * GROUP
-        for k in range(STEPS):
+        for parity in range(SPAN // GROUP):
+            pl.when(lax.rem(group, SPAN // GROUP) == parity)(functools.partial(arrivals, lax.div(t, SPAN), parity))
+
+        def load_amp(k, carry):
             amps[k] = jnp.broadcast_to(slabs_at(t + 1, HALO + k)[:, 0:1], (GROUP, LANES))
-        for r in range(edge, TALL - edge):
-            here[r] = slabs_at(t, r)
+            return carry
+
+        lax.fori_loop(0, STEPS, load_amp, 0, unroll=2)
+
+        def load_rows(i, carry):
+            for r in range(GROUP):
+                here[i * GROUP + r] = slabs_at(t, i * GROUP + r)
+            return carry
+
+        lax.fori_loop(0, TALL // GROUP, load_rows, 0)
 
         def two_steps(k, carry):
-            fine_step(here, there, 2 * k, edge + 1, TALL - edge - 1)
-            fine_step(there, here, 2 * k + 1, edge + 1, TALL - edge - 1)
+            fine_step(here, there, 2 * k)
+            fine_step(there, here, 2 * k + 1)
             return carry
 
         lax.fori_loop(0, STEPS // 2, two_steps, 0)
-        for r in range(edge + STEPS, TALL - edge - STEPS):
-            residual[group, (r - STEPS) * GROUP : (r - STEPS + 1) * GROUP] = here[r] - slabs_at(t + 1, r)
+
+        def finish(i, carry):
+            for r in range(GROUP):
+                row = i * GROUP + r
+                residual[group, pl.ds(pl.multiple_of(row * GROUP, GROUP), GROUP), :] = here[STEPS + row] - slabs_at(t + 1, STEPS + row)
+            return carry
+
+        lax.fori_loop(0, TRIM // GROUP, finish, 0)
+        return carry
 
     def back_copy(source, target):
         return pltpu.make_async_remote_copy(
@@ -274,32 +323,41 @@
     half = ROWS // 2
     lane_half = lanes_of((half, LANES))
 
-    def coarse_at(i):
-        return jnp.stack([coarse[i, pl.ds(b, 8, stride=8), :] for b in range(8)])
-
-    def sweep(group, place, e):
-        t = group * GROUP + place
-        up = jnp.concatenate([pltpu.roll(e[-1:], 1, 1), e[:-1]], axis=0)
-        down = jnp.concatenate([e[1:], pltpu.roll(e[:1], 7, 1)], axis=0)
-        add = jnp.stack([residual[group, pl.ds(b * GROUP + place, 8, stride=8 * GROUP), :] for b in range(8)])
-        e = coarse_at(0) * e + coarse_at(1) * (up + pltpu.roll(e, 1, 2)) + coarse_at(2) * (down + pltpu.roll(e, LANES - 1, 2)) + add
-        for b in range(8):
-            error[t, pl.ds(b, 8, stride=8), :] = e[b]
-        both = jnp.where(
-            lane_half < OWN,
-            pltpu.roll(error[t, SPAN : SPAN + half, :], LANES - SIDE, 1),
-            pltpu.roll(error[t, SPAN + half : SPAN + ROWS, :], SIDE, 1),
-        )
-
-        @pl.when(t == tm)
-        def _():
-            arrived[t] = both
-
-        @pl.when(t != tm)
-        def _():
-            packed[t] = both
-            back_copy(tm, t).start()
-
+    def sweep(group, e):
+        centre, c_up, c_down = ([coarse[i, pl.ds(STEPS + b, 8, stride=8), :] for b in range(8)] for i in range(3))
+
+        def step(place, e):
+            t = group * GROUP + place
+            above = [pltpu.roll(e[7], 1, 0)] + e[:7]
+            below = e[1:] + [pltpu.roll(e[0], 7, 0)]
+            after = []
+            for b in range(8):
+                up_left = above[b] + pltpu.roll(e[b], 1, 1)
+                down_right = below[b] + pltpu.roll(e[b], LANES - 1, 1)
+                add = residual[group, pl.ds(b * GROUP + place, 8, stride=8 * GROUP), :]
+                after.append(centre[b] * e[b] + c_up[b] * up_left + c_down[b] * down_right + add)
+            for b in range(8):
+                error[t, pl.ds(b, 8, stride=8), :] = after[b]
+            return after
+
+        e = lax.fori_loop(0, GROUP, step, e, unroll=2)
+
+        def pack(place, carry):
+            t = group * GROUP + place
+            top, bottom = error[t, SPAN : SPAN + half, :], error[t, SPAN + half : SPAN + ROWS, :]
+            packed[t] = jnp.where(lane_half < OWN, pltpu.roll(top, LANES - SIDE, 1), pltpu.roll(bottom, SIDE, 1))
+            return carry
+
+        lax.fori_loop(0, GROUP, pack, 0, unroll=4)
+
+        def give(t, carry):
+            @pl.when(t != tm)
+            def _():
+                back_copy(tm, t).start()
+
+            return carry
+
+        lax.fori_loop(group * GROUP, (group + 1) * GROUP, give, 0)
         return e
 
     edge_rows = {-1: (pl.ds(SPAN, SPAN), pl.ds(SPAN + ROWS, SPAN)), 1: (pl.ds(ROWS, SPAN), pl.ds(0, SPAN)), 0: (pl.ds(SPAN, ROWS), pl.ds(SPAN, ROWS))}
@@ -328,57 +386,58 @@
     row_trim = lax.broadcasted_iota(jnp.int32, (TRIM, LANES), 0)
     centre = (row_trim >= SPAN) & (row_trim < SPAN + ROWS)
 
-    e = jnp.zeros((8, 8, LANES), jnp.float32)
-    for s in range(stages):
-        for first, last, width in widths:
-            first, last = max(first, s * SPAN + 1), min(last, (s + 1) * SPAN + 1)
-            if first < last:
-                lax.fori_loop(first, last, functools.partial(arrive, width), 0)
-        for part in range(SPAN // GROUP):
-            relax(s * (SPAN // GROUP) + part, part * GROUP)
-        if s > 0:
+    groups = SPAN // GROUP
+    starts[...] = jnp.zeros((TRIM, LANES), jnp.float32)
+
+    def stage(s, carry):
+        lax.fori_loop(s * groups, (s + 1) * groups, relax, 0)
+
+        @pl.when(s > 0)
+        def _():
             for dz, copy in edge_copies(s - 1):
                 when_dz(dz, False, copy.wait_recv)
             left = pltpu.roll(edges[s - 1, 0], OWN, 1)
             right = pltpu.roll(edges[s - 1, 2], OWN, 1)
             own = jnp.where(centre, error[s * SPAN - 1], edges[s - 1, 1])
-            edges[s - 1, 1] = jnp.where(lane_trim < SIDE, left, jnp.where(lane_trim >= LANES - SIDE, right, own))
-            e = jnp.stack([edges[s - 1, 1, pl.ds(b, 8, stride=8), :] for b in range(8)])
-        for part in range(SPAN // GROUP):
-            e = lax.fori_loop(0, GROUP, functools.partial(sweep, s * (SPAN // GROUP) + part), e)
-        if s < stages - 1:
-            for slot in range(3):
-                @pl.when(jnp.logical_not(has_up))
-                def _():
-                    edges[s, slot, :SPAN, :] = jnp.zeros((SPAN, LANES), jnp.float32)
-
-                @pl.when(jnp.logical_not(has_down))
-                def _():
-                    edges[s, slot, SPAN + ROWS :, :] = jnp.zeros((SPAN, LANES), jnp.float32)
-
+            starts[...] = jnp.where(lane_trim < SIDE, left, jnp.where(lane_trim >= LANES - SIDE, right, own))
+
+        e = [starts[pl.ds(b, 8, stride=8), :] for b in range(8)]
+        lax.fori_loop(s * groups, (s + 1) * groups, sweep, e)
+
+        @pl.when(s < stages - 1)
+        def _():
             for dz, copy in edge_copies(s):
                 when_dz(dz, True, copy.start)
 
+        return carry
+
+    lax.fori_loop(0, stages, stage, 0)
+
     def sent(k, carry):
         window_copy(tm, lax.rem(tm + k, nt)).wait_send()
         return carry
 
     lax.fori_loop(1, nt, sent, 0)
 
-    def drain(copy, first, last, width):
-        lax.fori_loop(max(first, 1), last, lambda t, carry: (copy(t, width).wait_send(), carry)[1], 0)
+    def drain(copy):
+        def drain_stage(s, carry):
+            for first, last, width in widths:
+                lax.fori_loop(
+                    jnp.maximum(s * SPAN + first, 1), s * SPAN + last, lambda t, carry: (copy(t, width).wait_send(), carry)[1], 0
+                )
+            return carry
+
+        lax.fori_loop(0, nt // SPAN, drain_stage, 0)
 
     @pl.when(has_up)
     def _():
         params_up().wait_send()
-        for span in widths:
-            drain(state_up, *span)
+        drain(state_up)
 
     @pl.when(has_down)
     def _():
         params_down().wait_send()
-        for span in widths:
-            drain(state_down, *span)
+        drain(state_down)
 
     for s in range(stages - 1):
         for dz, copy in edge_copies(s):
@@ -400,7 +459,8 @@
         out_ref[0, half:, columns] = guess[half:, columns] + bottom
         return carry
 
-    lax.fori_loop(0, tiles, join, 0)
+    arrived[tm] = packed[tm]
+    lax.fori_loop(0, tiles, join, 0, unroll=4)
 
 
 def per_device(initial_state, guesses, diffusivity, forcing_field, amplitudes):
@@ -422,7 +482,7 @@
             vmem((nt, rows, LANES)),
             vmem((3, TALL, LANES)),
             vmem(((nt + 1) * TALL, LANES)),
-            vmem((3, TRIM, LANES)),
+            vmem((3, TALL, LANES)),
             vmem((4, TALL, GROUP, LANES)),
             vmem((STEPS, GROUP, LANES)),
             vmem((TALL, GROUP, LANES)),
@@ -430,6 +490,7 @@
             vmem((nt // GROUP, TRIM * GROUP, LANES)),
             vmem((nt, TRIM, LANES)),
             vmem((stages - 1, 3, TRIM, LANES)),
+            vmem((TRIM, LANES)),
             vmem((nt, rows // 2, LANES)),
             vmem((nt, rows // 2, LANES)),
             dma, dma, dma((3, 2)), dma((nt,)), dma((nt,)), dma((2,)), dma((2,)), dma((2, nt + 1)), dma((2, nt + 1)),

time: 44.4 us -> 42.5 us (0.957)
  the two profiles are of different devices: /device:TPU:95 before, /device:TPU:89 now
where the time goes in v3:
time: 42.5 us; the launch traced here: 41.8 us
  Pallas kernels  40.1 us (94%)
  local copies, waits for them, and re-layouts  1.67 us (4%)
    pallas_call x1, Pallas kernels, per_device(): pl.pallas_call(functools.partial(kernel, nt, nz), out_shape=jax.ShapeDtyp...  40.1 us
    unnamed x1, local copies, waits for them, and re-layouts  1.67 us

profile of v3, /device:TPU:89, one launch (start us, length us, event | category | flops | bytes accessed | tf_op | source)
XLA Modules:
  0.0 41.8 jit_solution(12445235371167478529)
XLA Ops:
  0.0 40.1 %shard_map.55 = f32[1,32,2048]{2,1,0:T(8,128)} custom-call(f32[32,2048]{1,0:T(8,128)} %initial_hbm.1, f32[1,32,2048]{2,1,0:T(8,128)} %guess_hbm.1, f32[32,2048]{1,0:T(8,128)} %kappa_hbm.1, f32[32,2048]{1,0:T(8,128)} %forcing_hbm.1, f32[8]{0:T(128)} %amp_hbm.1), custom_call_target="tpu_custom_call" | custom-call | tf_op jit(solution)/shard_map/pallas_call | solution.py:473
  40.1 1.7 %copy.7 = f32[1,32,2048]{2,1,0:T(8,128)} copy(f32[1,32,2048]{2,1,0:T(8,128)} %shard_map.55) | data formatting | bytes 524288

commit v4 on v3

--- a/solution.py
+++ b/solution.py
@@ -17,6 +17,8 @@
 TALL = ROWS + 2 * HALO
 TRIM = TALL - 2 * STEPS
 GROUP = 8
+PAIR = SPAN // GROUP
+CORE = ROWS - 2 * STEPS
 BLOCK = 6
 SIDE = 32
 OWN = LANES - 2 * SIDE
@@ -42,7 +44,7 @@
 
 def kernel(
     nt, nz, initial_hbm, guess_hbm, kappa_hbm, forcing_hbm, amp_hbm, out_ref,
-    amp_ref, guess, pairs, windows, params, states, coarse, fine, amps, here, there, residual, error, edges, starts, packed, arrived,
+    amp_ref, guess, pairs, windows, params, body, high, low, coarse, fine, amps, inner, inner_next, border, core, outer, outer_next, residual, error, edges, starts, packed, arrived,
     amp_sem, load_sem, pair_sem, win_send, win_recv, par_send, par_recv, z_send, z_recv, edge_send, edge_recv, back_send, back_recv,
 ):
     tm, z = lax.axis_index("tm"), lax.axis_index("space")
@@ -86,22 +88,25 @@
     for load in loads:
         load.start()
 
-    def state_rows(t, first, count):
-        return pl.ds(pl.multiple_of(t * TALL + first, 8), count)
-
-    def clear(first, t, carry):
-        states[state_rows(t, first, HALO), :] = jnp.zeros((HALO, LANES), jnp.float32)
+    def body_rows(t, first, count):
+        return pl.ds(pl.multiple_of(t * ROWS + first, 8), count)
+
+    def halo_rows(t, first, count):
+        return pl.ds(pl.multiple_of(t * HALO + first, 8), count)
+
+    def clear(ref, t, carry):
+        ref[halo_rows(t, 0, HALO), :] = jnp.zeros((HALO, LANES), jnp.float32)
         return carry
 
     @pl.when(jnp.logical_not(has_up))
     def _():
         params[:, :HALO, :] = jnp.zeros((3, HALO, LANES), jnp.float32)
-        lax.fori_loop(0, nt + 1, functools.partial(clear, 0), 0)
+        lax.fori_loop(0, nt + 1, functools.partial(clear, high), 0)
 
     @pl.when(jnp.logical_not(has_down))
     def _():
         params[:, HALO + ROWS :, :] = jnp.zeros((3, HALO, LANES), jnp.float32)
-        lax.fori_loop(0, nt + 1, functools.partial(clear, HALO + ROWS), 0)
+        lax.fori_loop(0, nt + 1, functools.partial(clear, low), 0)
 
     @pl.when(jnp.logical_not(has_up))
     def _():
@@ -137,7 +142,7 @@
 
     def window_copy(source, target):
         return pltpu.make_async_remote_copy(
-            windows.at[target], states.at[state_rows(source + 1, HALO, ROWS)], win_send.at[target], win_recv.at[source],
+            windows.at[target], body.at[body_rows(source + 1, 0, ROWS)], win_send.at[target], win_recv.at[source],
             device_id=(target, z), device_id_type=MESH,
         )
 
@@ -146,16 +151,16 @@
         return carry
 
     lax.fori_loop(1, nt, send_window, 0)
-    states[state_rows(tm + 1, HALO, ROWS), :] = windows[tm]
+    body[body_rows(tm + 1, 0, ROWS), :] = windows[tm]
 
     for load in loads:
         load.wait()
     shift = jnp.where(lax.rem(tm, 2) == 0, SIDE, LANES - SIDE)
     for i in range(3):
-        low, high = pltpu.roll(pairs[i, 0], shift, 1), pltpu.roll(pairs[i, 1], shift, 1)
-        value = jnp.where(lane < shift, low, high)
+        lower, upper = pltpu.roll(pairs[i, 0], shift, 1), pltpu.roll(pairs[i, 1], shift, 1)
+        value = jnp.where(lane < shift, lower, upper)
         if i == 0:
-            states[HALO : HALO + ROWS, :] = value
+            body[:ROWS, :] = value
         params[i, HALO : HALO + ROWS, :] = value
 
     def params_up():
@@ -172,13 +177,13 @@
 
     def state_up(t, width):
         return pltpu.make_async_remote_copy(
-            states.at[state_rows(t, HALO, width)], states.at[state_rows(t, HALO + ROWS, width)], z_send.at[0, t], z_recv.at[0, t],
+            body.at[body_rows(t, 0, width)], low.at[halo_rows(t, 0, width)], z_send.at[0, t], z_recv.at[0, t],
             device_id=(tm, z - 1), device_id_type=MESH,
         )
 
     def state_down(t, width):
         return pltpu.make_async_remote_copy(
-            states.at[state_rows(t, HALO + ROWS - width, width)], states.at[state_rows(t, HALO - width, width)], z_send.at[1, t], z_recv.at[1, t],
+            body.at[body_rows(t, ROWS - width, width)], high.at[halo_rows(t, HALO - width, width)], z_send.at[1, t], z_recv.at[1, t],
             device_id=(tm, z + 1), device_id_type=MESH,
         )
 
@@ -216,18 +221,7 @@
     def _():
         window_copy(nt - 1, tm).wait_recv()
 
-    @pl.when(has_down)
-    def _():
-        params_up().wait_recv()
-
-    @pl.when(has_up)
-    def _():
-        params_down().wait_recv()
-
-    states[:HALO, :] = params[0, :HALO, :]
-    states[HALO + ROWS : TALL, :] = params[0, HALO + ROWS :, :]
-
-    def factors(i, carry):
+    def factors(i):
         rows = pl.ds(pl.multiple_of(i * GROUP, GROUP), GROUP)
         row = i * GROUP + lax.broadcasted_iota(jnp.int32, (GROUP, LANES), 0)
         inside = ((row >= HALO) | has_up) & ((row < HALO + ROWS) | has_down)
@@ -241,78 +235,168 @@
                     coarse[k, rows, :] = value
         forcing = jnp.where(inside, params[2, rows, :], 0.0)
         fine[3, rows] = jnp.broadcast_to(forcing[:, None, :], (GROUP, GROUP, LANES))
-        return carry
-
-    lax.fori_loop(0, TALL // GROUP, factors, 0)
-
-    def arrive(width, t, carry):
-        @pl.when(has_down)
-        def _():
-            state_up(t, width).wait_recv()
-
-        @pl.when(has_up)
-        def _():
-            state_down(t, width).wait_recv()
-
-        return carry
-
-    def slabs_at(t, r):
-        return states[pl.ds(t * TALL + r, GROUP, stride=TALL), :]
-
-    def fine_step(source, target, k):
-        amp = amps[k]
-        for r in range(1, TALL - 1, BLOCK):
-            end = min(r + BLOCK, TALL - 1)
-            u = source[r - 1 : end + 1]
+
+    def own_factors(i, carry):
+        factors(HALO // GROUP + i)
+        return carry
+
+    lax.fori_loop(0, ROWS // GROUP, own_factors, 0)
+
+    def body_at(t, r):
+        return body[pl.ds(t * ROWS + r, GROUP, stride=ROWS), :]
+
+    def halo_at(ref, t, r):
+        return ref[pl.ds(t * HALO + r, GROUP, stride=HALO), :]
+
+    def advance(load, store, amp, first, count):
+        for r in range(0, count, BLOCK):
+            n = min(BLOCK, count - r)
+            u = load(r, n + 2)
             mid = u[1:-1]
             up_left = u[:-2] + pltpu.roll(mid, 1, 2)
             down_right = u[2:] + pltpu.roll(mid, LANES - 1, 2)
-            target[r:end] = fine[0, r:end] * mid + fine[1, r:end] * up_left + fine[2, r:end] * down_right + amp * fine[3, r:end]
-
-    def arrivals(s, parity):
-        first = parity * GROUP + 1
-        for place in range(first, first + GROUP):
-            width = width_of(place % SPAN)
-            if place > first and width == width_of((place - 1) % SPAN):
-                continue
-            last = place
-            while last < first + GROUP and width_of(last % SPAN) == width:
-                last += 1
-            lax.fori_loop(s * SPAN + place, jnp.minimum(s * SPAN + last, nt), functools.partial(arrive, width), 0)
-
-    def relax(group, carry):
-        t = group * GROUP
-        for parity in range(SPAN // GROUP):
-            pl.when(lax.rem(group, SPAN // GROUP) == parity)(functools.partial(arrivals, lax.div(t, SPAN), parity))
-
-        def load_amp(k, carry):
-            amps[k] = jnp.broadcast_to(slabs_at(t + 1, HALO + k)[:, 0:1], (GROUP, LANES))
+            centre, c_up, c_down, forcing = (fine[i, pl.ds(first + r, n)] for i in range(4))
+            store(r, n, centre * mid + c_up * up_left + c_down * down_right + amp * forcing)
+
+    def inner_step(source, target, s, k):
+        for g in range(PAIR):
+            border[s, g, k, 0:2] = source[g, pl.ds(k, 2)]
+            border[s, g, k, 2:4] = source[g, pl.ds(ROWS - 2 - k, 2)]
+
+            def load(r, n):
+                return source[g, r : r + n]
+
+            def store(r, n, value):
+                target[g, r + 1 : r + 1 + n] = value
+
+            advance(load, store, amps[s, g, k], HALO + 1, ROWS - 2)
+
+    def relax_inner(s, carry):
+        for g in range(PAIR):
+            t = s * SPAN + g * GROUP
+
+            def load_amp(k, carry):
+                amps[s, g, k] = jnp.broadcast_to(body_at(t + 1, k)[:, 0:1], (GROUP, LANES))
+                return carry
+
+            lax.fori_loop(0, STEPS, load_amp, 0, unroll=2)
+
+            def load_rows(i, carry):
+                for r in range(GROUP):
+                    inner[g, i * GROUP + r] = body_at(t, i * GROUP + r)
+                return carry
+
+            lax.fori_loop(0, ROWS // GROUP, load_rows, 0)
+
+        def two_steps(k, carry):
+            inner_step(inner, inner_next, s, 2 * k)
+            inner_step(inner_next, inner, s, 2 * k + 1)
             return carry
 
-        lax.fori_loop(0, STEPS, load_amp, 0, unroll=2)
-
-        def load_rows(i, carry):
-            for r in range(GROUP):
-                here[i * GROUP + r] = slabs_at(t, i * GROUP + r)
+        lax.fori_loop(0, STEPS // 2, two_steps, 0)
+        for g in range(PAIR):
+            core[s, g] = inner[g, STEPS : STEPS + CORE]
+        return carry
+
+    lax.fori_loop(0, nt // SPAN, relax_inner, 0)
+
+    @pl.when(has_down)
+    def _():
+        params_up().wait_recv()
+
+    @pl.when(has_up)
+    def _():
+        params_down().wait_recv()
+
+    high[:HALO, :] = params[0, :HALO, :]
+    low[:HALO, :] = params[0, HALO + ROWS :, :]
+
+    def halo_factors(i, carry):
+        factors(jnp.where(i < HALO // GROUP, i, i + ROWS // GROUP))
+        return carry
+
+    lax.fori_loop(0, 2 * HALO // GROUP, halo_factors, 0)
+
+    def arrive(width, t, carry):
+        @pl.when(has_down)
+        def _():
+            state_up(t, width).wait_recv()
+
+        @pl.when(has_up)
+        def _():
+            state_down(t, width).wait_recv()
+
+        return carry
+
+    def arrivals(s):
+        for first, last, width in widths:
+            lax.fori_loop(s * SPAN + max(first, 1), s * SPAN + last, functools.partial(arrive, width), 0)
+
+        @pl.when(s < nt // SPAN - 1)
+        def _():
+            arrive(HALO, (s + 1) * SPAN, 0)
+
+    def outer_step(source, target, s, k):
+        for g in range(PAIR):
+            for side in range(2):
+                def load(r, n):
+                    if side == 0 and r + n > HALO:
+                        return jnp.concatenate([source[g, 0, r:HALO], border[s, g, k, 0 : r + n - HALO]], axis=0)
+                    if side == 1 and r < 2:
+                        return jnp.concatenate([border[s, g, k, 2 + r : 4], source[g, 1, 0 : r + n - 2]], axis=0)
+                    first = r - 2 * side
+                    return source[g, side, first : first + n]
+
+                def store(r, n, value):
+                    target[g, side, r : r + n] = value
+
+                advance(load, store, amps[s, g, k], k + 1 if side == 0 else HALO + ROWS - 1 - k, HALO)
+
+    def relax(s):
+        arrivals(s)
+        for g in range(PAIR):
+            t = s * SPAN + g * GROUP
+
+            def load_rows(i, carry):
+                for r in range(GROUP):
+                    outer[g, 0, i * GROUP + r] = halo_at(high, t, i * GROUP + r)
+                    outer[g, 1, i * GROUP + r] = halo_at(low, t, i * GROUP + r)
+                return carry
+
+            lax.fori_loop(0, HALO // GROUP, load_rows, 0)
+
+        def two_steps(k, carry):
+            outer_step(outer, outer_next, s, 2 * k)
+            outer_step(outer_next, outer, s, 2 * k + 1)
             return carry
 
-        lax.fori_loop(0, TALL // GROUP, load_rows, 0)
-
-        def two_steps(k, carry):
-            fine_step(here, there, 2 * k)
-            fine_step(there, here, 2 * k + 1)
-            return carry
-
         lax.fori_loop(0, STEPS // 2, two_steps, 0)
 
-        def finish(i, carry):
-            for r in range(GROUP):
-                row = i * GROUP + r
-                residual[group, pl.ds(pl.multiple_of(row * GROUP, GROUP), GROUP), :] = here[STEPS + row] - slabs_at(t + 1, STEPS + row)
-            return carry
-
-        lax.fori_loop(0, TRIM // GROUP, finish, 0)
-        return carry
+        for g in range(PAIR):
+            t = s * SPAN + g * GROUP
+
+            def put(row, value):
+                residual[s * PAIR + g, pl.ds(pl.multiple_of((row - STEPS) * GROUP, GROUP), GROUP), :] = value
+
+            def finish_halo(i, carry):
+                for r in range(GROUP):
+                    row = i * GROUP + r
+                    put(STEPS + row, outer[g, 0, row] - halo_at(high, t + 1, STEPS + row))
+                    put(HALO + ROWS + row, outer[g, 1, STEPS + row] - halo_at(low, t + 1, row))
+                return carry
+
+            lax.fori_loop(0, (HALO - STEPS) // GROUP, finish_halo, 0)
+            for r in range(STEPS):
+                put(HALO + r, outer[g, 0, HALO - STEPS + r] - body_at(t + 1, r))
+                put(HALO + ROWS - STEPS + r, outer[g, 1, r] - body_at(t + 1, ROWS - STEPS + r))
+
+            def finish_core(i, carry):
+                for r in range(GROUP):
+                    row = i * GROUP + r
+                    put(HALO + STEPS + row, core[s, g, row] - body_at(t + 1, STEPS + row))
+                return carry
+
+            lax.fori_loop(0, CORE // GROUP, finish_core, 0)
 
     def back_copy(source, target):
         return pltpu.make_async_remote_copy(
@@ -390,7 +474,7 @@
     starts[...] = jnp.zeros((TRIM, LANES), jnp.float32)
 
     def stage(s, carry):
-        lax.fori_loop(s * groups, (s + 1) * groups, relax, 0)
+        relax(s)
 
         @pl.when(s > 0)
         def _():
@@ -481,12 +565,18 @@
             vmem((3, 2, rows, LANES)),
             vmem((nt, rows, LANES)),
             vmem((3, TALL, LANES)),
-            vmem(((nt + 1) * TALL, LANES)),
+            vmem(((nt + 1) * ROWS, LANES)),
+            vmem(((nt + 1) * HALO, LANES)),
+            vmem(((nt + 1) * HALO, LANES)),
             vmem((3, TALL, LANES)),
             vmem((4, TALL, GROUP, LANES)),
-            vmem((STEPS, GROUP, LANES)),
-            vmem((TALL, GROUP, LANES)),
-            vmem((TALL, GROUP, LANES)),
+            vmem((nt // SPAN, PAIR, STEPS, GROUP, LANES)),
+            vmem((PAIR, ROWS, GROUP, LANES)),
+            vmem((PAIR, ROWS, GROUP, LANES)),
+            vmem((nt // SPAN, PAIR, STEPS, 4, GROUP, LANES)),
+            vmem((nt // SPAN, PAIR, CORE, GROUP, LANES)),
+            vmem((PAIR, 2, HALO, GROUP, LANES)),
+            vmem((PAIR, 2, HALO, GROUP, LANES)),
             vmem((nt // GROUP, TRIM * GROUP, LANES)),
             vmem((nt, TRIM, LANES)),
             vmem((stages - 1, 3, TRIM, LANES)),

time: 42.5 us -> 41.8 us (0.984)
  no operation moved by 1% of the time
where the time goes in v4:
time: 41.8 us; the launch traced here: 41.5 us
  Pallas kernels  39.9 us (95%)
  local copies, waits for them, and re-layouts  1.67 us (4%)
    pallas_call x1, Pallas kernels, per_device(): pl.pallas_call(functools.partial(kernel, nt, nz), out_shape=jax.ShapeDtyp...  39.9 us
    unnamed x1, local copies, waits for them, and re-layouts  1.67 us

profile of v4, /device:TPU:89, one launch (start us, length us, event | category | flops | bytes accessed | tf_op | source)
XLA Modules:
  0.0 41.5 jit_solution(7022387443376935297)
XLA Ops:
  0.0 39.9 %shard_map.55 = f32[1,32,2048]{2,1,0:T(8,128)} custom-call(f32[32,2048]{1,0:T(8,128)} %initial_hbm.1, f32[1,32,2048]{2,1,0:T(8,128)} %guess_hbm.1, f32[32,2048]{1,0:T(8,128)} %kappa_hbm.1, f32[32,2048]{1,0:T(8,128)} %forcing_hbm.1, f32[8]{0:T(128)} %amp_hbm.1), custom_call_target="tpu_custom_call" | custom-call | tf_op jit(solution)/shard_map/pallas_call | solution.py:557
  39.9 1.7 %copy.7 = f32[1,32,2048]{2,1,0:T(8,128)} copy(f32[1,32,2048]{2,1,0:T(8,128)} %shard_map.55) | data formatting | bytes 524288

commit v5 on v4

--- a/solution.py
+++ b/solution.py
@@ -20,8 +20,10 @@
 PAIR = SPAN // GROUP
 CORE = ROWS - 2 * STEPS
 BLOCK = 6
+ACROSS = 8
 SIDE = 32
 OWN = LANES - 2 * SIDE
+VMEM_LIMIT = 536 * 2**20 // 10
 
 
 def width_of(place):
@@ -36,6 +38,12 @@
         else:
             found.append([place, place + 1, width_of(place)])
     return found
+
+
+def window_of(device):
+    turn = lax.rem(lax.div(device, ACROSS), 2)
+    place = lax.rem(device, ACROSS)
+    return device - place + jnp.where(turn == 1, ACROSS - 1 - place, place)
 
 
 def lanes_of(shape):
@@ -51,7 +59,8 @@
     tiles = guess.shape[1] // LANES
     widths = spans()
     has_up, has_down = z > 0, z < nz - 1
-    before, after = lax.rem(tm + nt - 1, nt), lax.rem(tm + 1, nt)
+    mine = window_of(tm)
+    before, after = window_of(lax.rem(mine + nt - 1, nt)), window_of(lax.rem(mine + 1, nt))
 
     barrier = pltpu.get_barrier_semaphore()
 
@@ -78,7 +87,7 @@
     load_guess.start()
     load_amps = pltpu.make_async_copy(amp_hbm, amp_ref, amp_sem)
     load_amps.start()
-    first = lax.rem(lax.div(tm + nt - 1, 2), tiles)
+    first = lax.rem(lax.div(mine + nt - 1, 2), tiles)
     second = lax.rem(first + 1, tiles)
     loads = []
     for i, ref in enumerate((initial_hbm, kappa_hbm, forcing_hbm)):
@@ -142,7 +151,7 @@
 
     def window_copy(source, target):
         return pltpu.make_async_remote_copy(
-            windows.at[target], body.at[body_rows(source + 1, 0, ROWS)], win_send.at[target], win_recv.at[source],
+            windows.at[window_of(target)], body.at[body_rows(source + 1, 0, ROWS)], win_send.at[target], win_recv.at[source],
             device_id=(target, z), device_id_type=MESH,
         )
 
@@ -151,11 +160,11 @@
         return carry
 
     lax.fori_loop(1, nt, send_window, 0)
-    body[body_rows(tm + 1, 0, ROWS), :] = windows[tm]
+    body[body_rows(tm + 1, 0, ROWS), :] = windows[mine]
 
     for load in loads:
         load.wait()
-    shift = jnp.where(lax.rem(tm, 2) == 0, SIDE, LANES - SIDE)
+    shift = jnp.where(lax.rem(mine, 2) == 0, SIDE, LANES - SIDE)
     for i in range(3):
         lower, upper = pltpu.roll(pairs[i, 0], shift, 1), pltpu.roll(pairs[i, 1], shift, 1)
         value = jnp.where(lane < shift, lower, upper)
@@ -400,7 +409,7 @@
 
     def back_copy(source, target):
         return pltpu.make_async_remote_copy(
-            packed.at[target], arrived.at[source], back_send.at[target], back_recv.at[source],
+            packed.at[target], arrived.at[window_of(source)], back_send.at[target], back_recv.at[source],
             device_id=(target, z), device_id_type=MESH,
         )
 
@@ -424,15 +433,17 @@
                 error[t, pl.ds(b, 8, stride=8), :] = after[b]
             return after
 
-        e = lax.fori_loop(0, GROUP, step, e, unroll=2)
-
-        def pack(place, carry):
+        def pack(place):
             t = group * GROUP + place
             top, bottom = error[t, SPAN : SPAN + half, :], error[t, SPAN + half : SPAN + ROWS, :]
             packed[t] = jnp.where(lane_half < OWN, pltpu.roll(top, LANES - SIDE, 1), pltpu.roll(bottom, SIDE, 1))
-            return carry
-
-        lax.fori_loop(0, GROUP, pack, 0, unroll=4)
+
+        def pack_and_step(place, e):
+            pack(place - 1)
+            return step(place, e)
+
+        e = lax.fori_loop(1, GROUP, pack_and_step, step(0, e))
+        pack(GROUP - 1)
 
         def give(t, carry):
             @pl.when(t != tm)
@@ -543,7 +554,7 @@
         out_ref[0, half:, columns] = guess[half:, columns] + bottom
         return carry
 
-    arrived[tm] = packed[tm]
+    arrived[mine] = packed[tm]
     lax.fori_loop(0, tiles, join, 0, unroll=4)
 
 
@@ -586,7 +597,7 @@
             dma, dma, dma((3, 2)), dma((nt,)), dma((nt,)), dma((2,)), dma((2,)), dma((2, nt + 1)), dma((2, nt + 1)),
             dma((stages - 1, 3, 3)), dma((stages - 1, 3, 3)), dma((nt,)), dma((nt,)),
         ],
-        compiler_params=pltpu.CompilerParams(collective_id=0, has_side_effects=True, vmem_limit_bytes=60 * 2**20),
+        compiler_params=pltpu.CompilerParams(collective_id=0, has_side_effects=True, vmem_limit_bytes=VMEM_LIMIT),
     )(initial_state, guesses, diffusivity, forcing_field, amplitudes)
 
 

time: 41.8 us -> 40 us (0.957)
  Pallas kernels: 39.9 us -> 38.5 us
    pallas_call x1, Pallas kernels: 39.9 us -> 38.5 us  [per_device(): pl.pallas_call(functools.partial(kernel, nt, nz), out_shape=jax.ShapeDtyp...]
    unnamed x1 -> x3, local copies, waits for them, and re-layouts: 1.67 us -> 1.36 us
where the time goes in v5:
time: 40 us; the launch traced here: 39.9 us
  Pallas kernels  38.5 us (96%)
  local copies, waits for them, and re-layouts  1.36 us (3%)
    pallas_call x1, Pallas kernels, per_device(): pl.pallas_call(functools.partial(kernel, nt, nz), out_shape=jax.ShapeDtyp...  38.5 us
    unnamed x3, local copies, waits for them, and re-layouts  1.36 us

profile of v5, /device:TPU:89, one launch (start us, length us, event | category | flops | bytes accessed | tf_op | source)
XLA Modules:
  0.0 39.9 jit_solution(1122928456612334681)
XLA Ops:
  0.0 0.0 copy-start
  0.0 0.7 %copy-done = f32[8]{0:T(128)S(1)} copy-done((f32[8]{0:T(128)S(1)}, f32[8]{0:T(128)}, u32[]{:S(2)}) %copy-start) | copy-done | bytes 56
  0.7 38.5 %shard_map.55 = f32[1,32,2048]{2,1,0:T(8,128)S(1)} custom-call(f32[32,2048]{1,0:T(8,128)} %initial_hbm.1, f32[1,32,2048]{2,1,0:T(8,128)} %guess_hbm.1, f32[32,2048]{1,0:T(8,128)} %kappa_hbm.1, f32[32,2048]{1,0:T(8,128)} %forcing_hbm.1, f32[8]{0:T(128)S(1)} %copy-done), custom_call_target="tpu_custom_call" | custom-call | tf_op jit(solution)/shard_map/pallas_call | solution.py:568
  39.2 0.7 %copy.7 = f32[1,32,2048]{2,1,0:T(8,128)} copy(f32[1,32,2048]{2,1,0:T(8,128)S(1)} %shard_map.55) | data formatting | bytes 524288
Async XLA Ops:
  0.0 0.7 %copy-start = (f32[8]{0:T(128)S(1)}, f32[8]{0:T(128)}, u32[]{:S(2)}) copy-start(f32[8]{0:T(128)} %amp_hbm.1) | copy-start | bytes 100

commit v6 on v5

--- a/solution.py
+++ b/solution.py
@@ -19,7 +19,7 @@
 GROUP = 8
 PAIR = SPAN // GROUP
 CORE = ROWS - 2 * STEPS
-BLOCK = 6
+BLOCK = 8
 ACROSS = 8
 SIDE = 32
 OWN = LANES - 2 * SIDE
@@ -257,9 +257,9 @@
     def halo_at(ref, t, r):
         return ref[pl.ds(t * HALO + r, GROUP, stride=HALO), :]
 
-    def advance(load, store, amp, first, count):
-        for r in range(0, count, BLOCK):
-            n = min(BLOCK, count - r)
+    def advance(load, store, amp, first, begin, end):
+        for r in range(begin, end, BLOCK):
+            n = min(BLOCK, end - r)
             u = load(r, n + 2)
             mid = u[1:-1]
             up_left = u[:-2] + pltpu.roll(mid, 1, 2)
@@ -278,7 +278,7 @@
             def store(r, n, value):
                 target[g, r + 1 : r + 1 + n] = value
 
-            advance(load, store, amps[s, g, k], HALO + 1, ROWS - 2)
+            advance(load, store, amps[s, g, k], HALO + 1, 0, ROWS - 2)
 
     def relax_inner(s, carry):
         for g in range(PAIR):
@@ -359,7 +359,11 @@
                 def store(r, n, value):
                     target[g, side, r : r + n] = value
 
-                advance(load, store, amps[s, g, k], k + 1 if side == 0 else HALO + ROWS - 1 - k, HALO)
+                skip = g * GROUP
+                if side == 0:
+                    advance(load, store, amps[s, g, k], k + 1, skip, HALO)
+                else:
+                    advance(load, store, amps[s, g, k], HALO + ROWS - 1 - k, 0, HALO - skip)
 
     def relax(s):
         arrivals(s)
@@ -442,7 +446,13 @@
             pack(place - 1)
             return step(place, e)
 
-        e = lax.fori_loop(1, GROUP, pack_and_step, step(0, e))
+        e = lax.fori_loop(1, GROUP, pack_and_step, step(0, e), unroll=7)
+
+        @pl.when((lax.rem(group, PAIR) == PAIR - 1) & (group < nt // GROUP - 1))
+        def _():
+            for dz, copy in edge_copies(lax.div(group, PAIR)):
+                when_dz(dz, True, copy.start)
+
         pack(GROUP - 1)
 
         def give(t, carry):
@@ -499,11 +509,6 @@
         e = [starts[pl.ds(b, 8, stride=8), :] for b in range(8)]
         lax.fori_loop(s * groups, (s + 1) * groups, sweep, e)
 
-        @pl.when(s < stages - 1)
-        def _():
-            for dz, copy in edge_copies(s):
-                when_dz(dz, True, copy.start)
-
         return carry
 
     lax.fori_loop(0, stages, stage, 0)
@@ -555,7 +560,7 @@
         return carry
 
     arrived[mine] = packed[tm]
-    lax.fori_loop(0, tiles, join, 0, unroll=4)
+    lax.fori_loop(0, tiles, join, 0, unroll=8)
 
 
 def per_device(initial_state, guesses, diffusivity, forcing_field, amplitudes):

time: 40 us -> 39.1 us (0.978)
  Pallas kernels: 38.5 us -> 37.6 us
    pallas_call x1, Pallas kernels: 38.5 us -> 37.6 us  [per_device(): pl.pallas_call(functools.partial(kernel, nt, nz), out_shape=jax.ShapeDtyp...]
where the time goes in v6:
time: 39.1 us; the launch traced here: 39 us
  Pallas kernels  37.6 us (96%)
  local copies, waits for them, and re-layouts  1.36 us (3%)
    pallas_call x1, Pallas kernels, per_device(): pl.pallas_call(functools.partial(kernel, nt, nz), out_shape=jax.ShapeDtyp...  37.6 us
    unnamed x3, local copies, waits for them, and re-layouts  1.36 us

profile of v6, /device:TPU:89, one launch (start us, length us, event | category | flops | bytes accessed | tf_op | source)
XLA Modules:
  0.0 39.0 jit_solution(8466935893875590795)
XLA Ops:
  0.0 0.0 copy-start
  0.0 0.7 %copy-done = f32[8]{0:T(128)S(1)} copy-done((f32[8]{0:T(128)S(1)}, f32[8]{0:T(128)}, u32[]{:S(2)}) %copy-start) | copy-done | bytes 56
  0.7 37.6 %shard_map.55 = f32[1,32,2048]{2,1,0:T(8,128)S(1)} custom-call(f32[32,2048]{1,0:T(8,128)} %initial_hbm.1, f32[1,32,2048]{2,1,0:T(8,128)} %guess_hbm.1, f32[32,2048]{1,0:T(8,128)} %kappa_hbm.1, f32[32,2048]{1,0:T(8,128)} %forcing_hbm.1, f32[8]{0:T(128)S(1)} %copy-done), custom_call_target="tpu_custom_call" | custom-call | tf_op jit(solution)/shard_map/pallas_call | solution.py:573
  38.3 0.7 %copy.7 = f32[1,32,2048]{2,1,0:T(8,128)} copy(f32[1,32,2048]{2,1,0:T(8,128)S(1)} %shard_map.55) | data formatting | bytes 524288
Async XLA Ops:
  0.0 0.7 %copy-start = (f32[8]{0:T(128)S(1)}, f32[8]{0:T(128)}, u32[]{:S(2)}) copy-start(f32[8]{0:T(128)} %amp_hbm.1) | copy-start | bytes 100

commit v7 on v6

--- a/solution.py
+++ b/solution.py
@@ -468,7 +468,7 @@
     edge_rows = {-1: (pl.ds(SPAN, SPAN), pl.ds(SPAN + ROWS, SPAN)), 1: (pl.ds(ROWS, SPAN), pl.ds(0, SPAN)), 0: (pl.ds(SPAN, ROWS), pl.ds(SPAN, ROWS))}
 
     def edge_copies(s):
-        for dz in (-1, 0, 1):
+        for dz in (-1, 1, 0):
             for slot, target in ((2, before), (1, tm), (0, after)):
                 if dz == 0 and slot == 1:
                     continue

time: 39.1 us -> 39.1 us (level)
  no operation moved by 1% of the time
where the time goes in v7:
time: 39.1 us; the launch traced here: 39 us
  Pallas kernels  37.6 us (96%)
  local copies, waits for them, and re-layouts  1.36 us (3%)
    pallas_call x1, Pallas kernels, per_device(): pl.pallas_call(functools.partial(kernel, nt, nz), out_shape=jax.ShapeDtyp...  37.6 us
    unnamed x3, local copies, waits for them, and re-layouts  1.36 us

profile of v7, /device:TPU:89, one launch (start us, length us, event | category | flops | bytes accessed | tf_op | source)
XLA Modules:
  0.0 39.0 jit_solution(5679354525026496711)
XLA Ops:
  0.0 0.0 copy-start
  0.0 0.7 %copy-done = f32[8]{0:T(128)S(1)} copy-done((f32[8]{0:T(128)S(1)}, f32[8]{0:T(128)}, u32[]{:S(2)}) %copy-start) | copy-done | bytes 56
  0.7 37.6 %shard_map.55 = f32[1,32,2048]{2,1,0:T(8,128)S(1)} custom-call(f32[32,2048]{1,0:T(8,128)} %initial_hbm.1, f32[1,32,2048]{2,1,0:T(8,128)} %guess_hbm.1, f32[32,2048]{1,0:T(8,128)} %kappa_hbm.1, f32[32,2048]{1,0:T(8,128)} %forcing_hbm.1, f32[8]{0:T(128)S(1)} %copy-done), custom_call_target="tpu_custom_call" | custom-call | tf_op jit(solution)/shard_map/pallas_call | solution.py:573
  38.3 0.7 %copy.7 = f32[1,32,2048]{2,1,0:T(8,128)} copy(f32[1,32,2048]{2,1,0:T(8,128)S(1)} %shard_map.55) | data formatting | bytes 524288
Async XLA Ops:
  0.0 0.7 %copy-start = (f32[8]{0:T(128)S(1)}, f32[8]{0:T(128)}, u32[]{:S(2)}) copy-start(f32[8]{0:T(128)} %amp_hbm.1) | copy-start | bytes 100
